TPU v7x, 256 devices: a whole 4x4x8 slice. The times are simulated.
256 devices in a mesh: seq: 64 (over y, z, core), mp: 4 (over x).
Axes of the slice: x: 4, y: 4, z: 8, core: 2. Of those that a mesh axis runs over, the one named last changes fastest.
Arguments:
- queries: bfloat16 [512, 64, 4096], P('seq', None, 'mp'), may hold values from -5 to 5
- out_grad: bfloat16 [512, 64, 4096], P('seq', None, 'mp'), may hold values from -6 to 6
- row_keys: bfloat16 [512, 128, 4096], P('seq', None, 'mp'), may hold values from -5 to 5
- row_values: bfloat16 [512, 128, 4096], P('seq', None, 'mp'), may hold values from -6 to 6
- neighbours: int32 [512, 2], P(('seq', 'mp')), may hold values from 0 to 511, as said below
Outputs:
- query_grad: bfloat16 [512, 64, 4096], P('seq', None, 'mp')
- key_grad: bfloat16 [512, 128, 4096], P('seq', None, 'mp')
- value_grad: bfloat16 [512, 128, 4096], P('seq', None, 'mp')
Inputs may be any that keep to these rules, and one draw needn't show every extreme that they name: Row r lies with seq index r // 8. The 2 neighbours of a span are different rows. The spans of one seq index retrieve at most 1 row lying with any one seq index, and some seq indices are retrieved from that often by every seq index.
All inputs are finite; a program needn't handle non-finite values.
Results may differ from a plain program's by a relative error of at most 0.008.
Values may be sent and summed in bfloat16 or wider, within the bound.
A program may use at most 320 MiB of HBM per device.

v0:
```python
import jax
import jax.numpy as jnp
from jax import lax
from jax.sharding import PartitionSpec as P

HEAD = 128
SPAN = 64
NLEN = 128
NBR = 2


slot_group = 8


def split_heads(tensor):
    return tensor.reshape(tensor.shape[:-1] + (tensor.shape[-1] // HEAD, HEAD))


def per_device(queries, out_grad, row_keys, row_values, neighbours):
    seq_count = lax.axis_size("seq")
    own_lists = lax.all_gather(neighbours, "mp", axis=0, tiled=True)
    span_count = queries.shape[0]
    rows_here = row_keys.shape[0]
    width_here = queries.shape[2]
    heads_here = width_here // HEAD
    flat_rows = own_lists.reshape(-1)
    item_count = flat_rows.shape[0]
    owner_dev = flat_rows // rows_here
    local_row = flat_rows % rows_here
    slot_depth = (item_count + seq_count - 1) // seq_count
    slot_total = seq_count * slot_depth
    position = jnp.arange(item_count)
    same_before = (owner_dev[:, None] == owner_dev[None, :]) & (
        position[None, :] < position[:, None]
    )
    earlier = jnp.sum(same_before.astype(jnp.int32), axis=1)
    target = owner_dev * slot_depth + earlier
    item_span = position // NBR
    score_scale = HEAD ** (-0.5)
    row_send = jnp.zeros((slot_total,), jnp.int32).at[target].set(local_row)
    query_send = (
        jnp.zeros((slot_total,) + queries.shape[1:], queries.dtype)
        .at[target]
        .set(queries[item_span])
    )
    grad_send = (
        jnp.zeros((slot_total,) + out_grad.shape[1:], out_grad.dtype)
        .at[target]
        .set(out_grad[item_span])
    )
    query_recv, grad_recv, row_recv = (
        lax.all_to_all(query_send, "seq", split_axis=0, concat_axis=0, tiled=True),
        lax.all_to_all(grad_send, "seq", split_axis=0, concat_axis=0, tiled=True),
        lax.all_to_all(row_send, "seq", split_axis=0, concat_axis=0, tiled=True),
    )
    group_count = slot_total // slot_group

    def grouped(tensor):
        return tensor.reshape((group_count, slot_group) + tensor.shape[1:])

    def first_pass(block):
        query_block, grad_block, row_block = block
        query_heads = split_heads(query_block)
        grad_heads = split_heads(grad_block)
        key_heads = split_heads(row_keys[row_block])
        value_heads = split_heads(row_values[row_block])
        scores = (
            jnp.einsum(
                "bihd,bjhd->bhij", query_heads, key_heads, preferred_element_type=jnp.float32
            )
            * score_scale
        )
        highest = jnp.max(scores, axis=3)
        expons = jnp.exp(scores - highest[..., None])
        grad_p = jnp.einsum(
            "bihd,bjhd->bhij", grad_heads, value_heads, preferred_element_type=jnp.float32
        )
        return (highest, jnp.sum(expons, axis=3), jnp.sum(expons * grad_p, axis=3))

    part_max, part_sum, part_cross = lax.map(
        first_pass, (grouped(query_recv), grouped(grad_recv), grouped(row_recv))
    )
    stat_shape = (slot_total, heads_here * SPAN)
    part_max = part_max.reshape(stat_shape)
    part_sum = part_sum.reshape(stat_shape)
    part_cross = part_cross.reshape(stat_shape)
    back_max, back_sum, back_cross = (
        lax.all_to_all(part_max, "seq", split_axis=0, concat_axis=0, tiled=True),
        lax.all_to_all(part_sum, "seq", split_axis=0, concat_axis=0, tiled=True),
        lax.all_to_all(part_cross, "seq", split_axis=0, concat_axis=0, tiled=True),
    )

    def per_item(tensor):
        return tensor[target].reshape(span_count, NBR, heads_here * SPAN)

    item_max = per_item(back_max)
    item_sum = per_item(back_sum)
    item_cross = per_item(back_cross)
    span_max = jnp.max(item_max, axis=1, keepdims=True)
    factor = jnp.exp(item_max - span_max)
    span_sum = jnp.sum(item_sum * factor, axis=1)
    log_total = span_max[:, 0] + jnp.log(span_sum)
    row_delta = jnp.sum(item_cross * factor, axis=1) / span_sum
    norm_send = jnp.zeros(stat_shape, jnp.float32).at[target].set(log_total[item_span])
    delta_send = jnp.zeros(stat_shape, jnp.float32).at[target].set(row_delta[item_span])
    norm_recv, delta_recv = (
        lax.all_to_all(norm_send, "seq", split_axis=0, concat_axis=0, tiled=True),
        lax.all_to_all(delta_send, "seq", split_axis=0, concat_axis=0, tiled=True),
    )

    def second_pass(carry, block):
        key_acc, value_acc = carry
        query_block, grad_block, row_block, norm_block, delta_block = block
        query_heads = split_heads(query_block)
        grad_heads = split_heads(grad_block)
        key_heads = split_heads(row_keys[row_block])
        value_heads = split_heads(row_values[row_block])
        scores = (
            jnp.einsum(
                "bihd,bjhd->bhij", query_heads, key_heads, preferred_element_type=jnp.float32
            )
            * score_scale
        )
        norm_here = norm_block.reshape(slot_group, heads_here, SPAN)
        delta_here = delta_block.reshape(slot_group, heads_here, SPAN)
        softmax_p = jnp.exp(scores - norm_here[..., None])
        grad_p = jnp.einsum(
            "bihd,bjhd->bhij", grad_heads, value_heads, preferred_element_type=jnp.float32
        )
        grad_s = (softmax_p * (grad_p - delta_here[..., None]) * score_scale).astype(jnp.bfloat16)
        probs_low = softmax_p.astype(jnp.bfloat16)
        value_part = jnp.einsum(
            "bhij,bihd->bjhd", probs_low, grad_heads, preferred_element_type=jnp.float32
        )
        key_part = jnp.einsum(
            "bhij,bihd->bjhd", grad_s, query_heads, preferred_element_type=jnp.float32
        )
        query_part = jnp.einsum(
            "bhij,bjhd->bihd", grad_s, key_heads, preferred_element_type=jnp.float32
        )
        value_part = value_part.reshape(slot_group, NLEN, width_here)
        key_part = key_part.reshape(slot_group, NLEN, width_here)
        query_part = query_part.astype(jnp.bfloat16).reshape(slot_group, SPAN, width_here)
        return (
            (key_acc.at[row_block].add(key_part), value_acc.at[row_block].add(value_part)),
            query_part,
        )

    start = (
        jnp.zeros((rows_here, NLEN, width_here), jnp.float32),
        jnp.zeros((rows_here, NLEN, width_here), jnp.float32),
    )
    blocks = (
        grouped(query_recv),
        grouped(grad_recv),
        grouped(row_recv),
        grouped(norm_recv),
        grouped(delta_recv),
    )
    (key_acc, value_acc), query_parts = lax.scan(second_pass, start, blocks)
    query_parts = query_parts.reshape(slot_total, SPAN, width_here)
    query_back = lax.all_to_all(query_parts, "seq", split_axis=0, concat_axis=0, tiled=True)
    returned = query_back[target].reshape(span_count, NBR, SPAN, width_here).astype(jnp.float32)
    query_grad = jnp.sum(returned, axis=1).astype(jnp.bfloat16)
    return (query_grad, key_acc.astype(jnp.bfloat16), value_acc.astype(jnp.bfloat16))


def solution(mesh):
    in_specs = (
        P("seq", None, "mp"),
        P("seq", None, "mp"),
        P("seq", None, "mp"),
        P("seq", None, "mp"),
        P(("seq", "mp"), None),
    )
    out_specs = (P("seq", None, "mp"), P("seq", None, "mp"), P("seq", None, "mp"))
    return jax.shard_map(
        per_device, mesh=mesh, in_specs=in_specs, out_specs=out_specs, check_vma=False
    )
```

profile of v0, /device:TPU:1, one launch (start us, length us, event | category | flops | bytes accessed | tf_op | source)
XLA Modules:
  0.0 1276.6 jit_solution(1878538343176599695)
XLA Ops:
  0.6 8.9 all-gather
  11.3 14.3 %all-to-all-start = ((s32[64,1,1]{2,1,0:T(1,128)}), s32[64,1,1]{2,1,0:T(1,128)S(1)}, u32[]{:S(2)}, u32[]{:S(2)}) async-start(s32[64,1,1]{2,1,0:T(1,128)} %copy.75), calls=%async_computation | async-start | bytes 65536 | tf_op jit(solution)/shard_map/all_to_all | solution.py:54
  35.9 10.7 all-to-all-start.1
  56.8 175.5 %all-to-all-done.1 = bf16[64,64,1024]{2,1,0:T(8,128)(2,1)} async-done(((bf16[64,64,1024]{2,1,0:T(8,128)(2,1)}), bf16[64,64,1024]{2,1,0:T(8,128)(2,1)}, u32[]{:S(2)}, u32[]{:S(2)}) %all-to-all-start.1) | async-done | bytes 8388640 | tf_op jit(solution)/shard_map/all_to_all | solution.py:52
  232.3 6.1 all-to-all-start.2
  239.8 184.4 %all-to-all-done.2 = bf16[64,64,1024]{2,1,0:T(8,128)(2,1)} async-done(((bf16[64,64,1024]{2,1,0:T(8,128)(2,1)}), bf16[64,64,1024]{2,1,0:T(8,128)(2,1)}, u32[]{:S(2)}, u32[]{:S(2)}) %all-to-all-start.2) | async-done | bytes 8388640 | tf_op jit(solution)/shard_map/all_to_all | solution.py:53
  424.2 130.9 %while.28 = (s32[]{:T(128)}, f32[8,8,8,64]{3,2,1,0:T(8,128)}, f32[8,8,8,64]{3,2,1,0:T(8,128)}, f32[8,8,8,64]{3,2,1,0:T(8,128)S(1)}, bf16[8,8,64,1024]{3,2,1,0:T(...) while((s32[]{:T(128)}, f32[8,8,8,64]{3,2,1,0:T(8,128)}, ...), condition=%wide.region_8.9_spmd, body=%wide.region_4.8_spmd.sunk | while | flops 273142816 | bytes 42209624 | solution.py:80
  555.9 5.9 all-to-all-start.6
  563.6 8.6 all-to-all-done.6
  578.8 8.6 all-to-all-done.3
  593.7 9.1 all-to-all-done.4
  611.5 8.9 all-to-all-done.7
  625.3 10.3 all-to-all-done.5
  640.7 432.0 %while.29 = (s32[]{:T(128)}, f32[8,128,1024]{2,1,0:T(8,128)}, f32[8,128,1024]{2,1,0:T(8,128)}, bf16[8,8,64,1024]{3,2,1,0:T(8,128)(2,1)}, s32[8,8]{1,0:T(8,128)S(...) while((s32[]{:T(128)}, f32[8,128,1024]{2,1,0:T(8,128)}, ...), condition=%wide.region_17.18_spmd, body=%wide.region_14.17_spmd.sunk | while | flops 678429696 | bytes 136499760 | solution.py:160
  667.9 8.7 scatter_fusion.1
  684.7 8.9 scatter_fusion
  721.8 8.7 scatter_fusion.1
  738.6 8.9 scatter_fusion
  775.8 8.8 scatter_fusion.1
  792.7 8.9 scatter_fusion
  829.8 8.7 scatter_fusion.1
  846.7 8.9 scatter_fusion
  883.8 8.9 scatter_fusion.1
  900.8 9.0 scatter_fusion
  938.1 8.7 scatter_fusion.1
  954.9 8.8 scatter_fusion
  992.0 8.7 scatter_fusion.1
  1008.8 8.8 scatter_fusion
  1045.9 8.7 scatter_fusion.1
  1062.7 8.9 scatter_fusion
  1072.7 12.5 all-to-all-start.8
  1090.8 180.1 %all-to-all-done.8 = bf16[64,64,1024]{2,1,0:T(8,128)(2,1)} async-done(((bf16[64,64,1024]{2,1,0:T(8,128)(2,1)}), bf16[64,64,1024]{2,1,0:T(8,128)(2,1)}, u32[]{:S(2)}, u32[]{:S(2)}) %all-to-all-start.8) | async-done | bytes 8388640 | tf_op jit(solution)/shard_map/all_to_all | solution.py:162
  (470 shorter events, 489.4 us)
Async XLA Ops:
  0.6 25.0 %copy-start = (bf16[8,64,1024]{2,1,0:T(8,128)(2,1)S(1)}, bf16[8,64,1024]{2,1,0:T(8,128)(2,1)}, u32[]{:S(2)}) copy-start(bf16[8,64,1024]{2,1,0:T(8,128)(2,1)} %param.9) | copy-start | bytes 3145732
  11.3 24.6 %all-to-all-start = ((s32[64,1,1]{2,1,0:T(1,128)}), s32[64,1,1]{2,1,0:T(1,128)S(1)}, u32[]{:S(2)}, u32[]{:S(2)}) async-start(s32[64,1,1]{2,1,0:T(1,128)} %copy.75), calls=%async_computation | async-start | bytes 65536 | tf_op jit(solution)/shard_map/all_to_all | solution.py:54
  35.9 10.7 copy-start.12
  35.9 196.4 %all-to-all-start.1 = ((bf16[64,64,1024]{2,1,0:T(8,128)(2,1)}), bf16[64,64,1024]{2,1,0:T(8,128)(2,1)}, u32[]{:S(2)}, u32[]{:S(2)}) async-start(bf16[64,64,1024]{2,1,0:T(8,128)(2,1)} %scatter_fusion.2), calls=%async_computation.1 | async-start | bytes 16777216 | tf_op jit(solution)/shard_map/all_to_all | solution.py:52
  232.3 191.9 %all-to-all-start.2 = ((bf16[64,64,1024]{2,1,0:T(8,128)(2,1)}), bf16[64,64,1024]{2,1,0:T(8,128)(2,1)}, u32[]{:S(2)}, u32[]{:S(2)}) async-start(bf16[64,64,1024]{2,1,0:T(8,128)(2,1)} %scatter_fusion.3), calls=%async_computation.2 | async-start | bytes 16777216 | tf_op jit(solution)/shard_map/all_to_all | solution.py:53
  555.9 16.3 %all-to-all-start.6 = ((f32[64,1,512]{2,1,0:T(1,128)}), f32[64,1,512]{2,1,0:T(1,128)S(1)}, u32[]{:S(2)}, u32[]{:S(2)}) async-start(f32[64,1,512]{2,1,0:T(1,128)} %all_to_all.63), calls=%async_computation.6 | async-start | bytes 262144 | tf_op jit(solution)/shard_map/all_to_all | solution.py:90
  572.2 15.2 %all-to-all-start.3 = ((f32[64,1,512]{2,1,0:T(1,128)}), f32[64,1,512]{2,1,0:T(1,128)S(1)}, u32[]{:S(2)}, u32[]{:S(2)}) async-start(f32[64,1,512]{2,1,0:T(1,128)} %all_to_all.55), calls=%async_computation.3 | async-start | bytes 262144 | tf_op jit(solution)/shard_map/all_to_all | solution.py:88
  587.4 15.4 %all-to-all-start.4 = ((f32[64,1,512]{2,1,0:T(1,128)}), f32[64,1,512]{2,1,0:T(1,128)S(1)}, u32[]{:S(2)}, u32[]{:S(2)}) async-start(f32[64,1,512]{2,1,0:T(1,128)} %all_to_all.58), calls=%async_computation.4 | async-start | bytes 262144 | tf_op jit(solution)/shard_map/all_to_all | solution.py:89
  605.2 15.2 %all-to-all-start.7 = ((f32[64,1,512]{2,1,0:T(1,128)}), f32[64,1,512]{2,1,0:T(1,128)S(1)}, u32[]{:S(2)}, u32[]{:S(2)}) async-start(f32[64,1,512]{2,1,0:T(1,128)} %copy.76), calls=%async_computation.7 | async-start | bytes 262144 | tf_op jit(solution)/shard_map/all_to_all | solution.py:108
  620.4 15.2 %all-to-all-start.5 = ((f32[64,1,512]{2,1,0:T(1,128)}), f32[64,1,512]{2,1,0:T(1,128)S(1)}, u32[]{:S(2)}, u32[]{:S(2)}) async-start(f32[64,1,512]{2,1,0:T(1,128)} %all_to_all.61), calls=%async_computation.5 | async-start | bytes 262144 | tf_op jit(solution)/shard_map/all_to_all | solution.py:107
  653.9 4.0 copy-start.3
  667.9 8.7 copy-start.8
  684.7 8.9 copy-start.6
  707.9 4.0 copy-start.3
  721.8 8.7 copy-start.8
  738.6 8.9 copy-start.6
  775.8 8.8 copy-start.8
  792.7 8.9 copy-start.6
  815.9 4.0 copy-start.3
  829.8 8.8 copy-start.8
  846.7 8.9 copy-start.6
  869.9 4.0 copy-start.3
  883.8 8.9 copy-start.8
  900.8 9.0 copy-start.6
  938.1 8.7 copy-start.8
  954.9 8.9 copy-start.6
  992.0 8.7 copy-start.8
  1008.8 8.8 copy-start.6
  1045.9 8.7 copy-start.8
  1062.7 8.9 copy-start.6
  1072.7 198.3 %all-to-all-start.8 = ((bf16[64,64,1024]{2,1,0:T(8,128)(2,1)}), bf16[64,64,1024]{2,1,0:T(8,128)(2,1)}, u32[]{:S(2)}, u32[]{:S(2)}) async-start(bf16[64,64,1024]{2,1,0:T(8,128)(2,1)} %bitcast.209), calls=%async_computation.8 | async-start | bytes 16777216 | tf_op jit(solution)/shard_map/all_to_all | solution.py:162
  1270.9 5.7 copy-start.1
  (53 other events, 100.0 us)
where the time goes:
time: 1280 us
  waiting for transfers between devices  586 us (46%)
  local copies, waits for them, and re-layouts  331 us (26%)
  other arithmetic  161 us (13%)
  matrix products  120 us (9%)
  starting transfers between devices  69.2 us (5%)
    all_to_all x1, waiting for transfers between devices, per_device(): lax.all_to_all(grad_send, 'seq', split_axis=0, concat_axis=0, tiled=True)  184 us
    all_to_all x1, waiting for transfers between devices, per_device(): lax.all_to_all(query_parts, 'seq', split_axis=0, concat_axis=0, tiled=True)  180 us
    all_to_all x1, waiting for transfers between devices, per_device(): lax.all_to_all(query_send, 'seq', split_axis=0, concat_axis=0, tiled=True)  176 us
    scatter-add x8, other arithmetic, second_pass(): key_acc.at[row_block].add(key_part)  71.1 us
    scatter-add x8, other arithmetic, second_pass(): value_acc.at[row_block].add(value_part)  69.9 us
    reshape x8, local copies, waits for them, and re-layouts, second_pass(): value_part = value_part.reshape(slot_group, NLEN, width_here)  43.1 us
    reshape x8, local copies, waits for them, and re-layouts, second_pass(): key_part = key_part.reshape(slot_group, NLEN, width_here)  43.1 us
    dot_general x8, matrix products, second_pass(): jnp.einsum('bhij,bihd->bjhd', probs_low, grad_heads, preferred_element_ty...  36.2 us
  transfers between devices with their start and end apart: 9, of which 8 were waited for; matrix products, arithmetic and copies ran while one was open for 2% of the time, Pallas kernels for 0%

commit v1 on v0

v1 whole, which is shorter than its diff:
```python
import functools

import jax
import jax.numpy as jnp
from jax import lax
from jax.experimental import pallas as pl
from jax.experimental.pallas import tpu as pltpu
from jax.sharding import PartitionSpec as P

HEAD = 128
SPAN = 64
NLEN = 128
NBR = 2
NY, NZ, NC = 4, 8, 2
CH, ROWS = 8, 8
WIDE = 1024
HALF = WIDE // NC
PAIR = 2 * HEAD
PAIRS = HALF // PAIR
SOURCES = NZ * NC
SPANS_HERE = SOURCES * CH
ROWS_HERE = NY * NC * ROWS
SCALE = HEAD ** (-0.5)
LOWEST = -1e30
MESH = pl.DeviceIdType.MESH
ANY = pl.BlockSpec(memory_space=pl.ANY)
f32, bf16 = jnp.float32, jnp.bfloat16


def place():
    me = lax.axis_index("seq")
    core = lax.rem(me, NC)
    z = lax.rem(me // NC, NZ)
    y = me // (NC * NZ)
    return y, z, core


def index_of(y, z, core):
    return (lax.rem(y + NY, NY) * NZ + lax.rem(z + NZ, NZ)) * NC + core


def greet(peers):
    barrier = pltpu.get_barrier_semaphore()
    for peer in peers:
        pl.semaphore_signal(barrier, inc=1, device_id={"seq": peer}, device_id_type=MESH)
    pl.semaphore_wait(barrier, len(peers))


def remote(src, dst, send_sem, recv_sem, peer):
    return pltpu.make_async_remote_copy(
        src_ref=src, dst_ref=dst, send_sem=send_sem, recv_sem=recv_sem,
        device_id={"seq": peer}, device_id_type=MESH)


def gather_kernel(q, g, k, v, qa, ga, ka, va, loc, sib_s, sib_r, zs, zr, ys, yr):
    y, z, core = place()
    sib = index_of(y, z, 1 - core)
    z_peer = (index_of(y, z + 1, core), index_of(y, z - 1, core))
    y_peer = (index_of(y + 1, z, core), index_of(y - 1, z, core))
    greet((sib,) + z_peer + y_peer)
    own = pl.ds(pl.multiple_of(core * HALF, HALF), HALF)
    other = pl.ds(pl.multiple_of((1 - core) * HALF, HALF), HALF)
    sources = (q, g, k, v)
    gathered = (qa, ga, ka, va)
    at = (z, z, y, y)

    def z_copy(d, sub, t):
        part = core if sub == 0 else 1 - core
        block = lax.rem(z - t + NZ, NZ) if d == 0 else lax.rem(z + t, NZ)
        dst = gathered[d].at[block, part]
        src = sources[d].at[:, :, own] if (t == 0 and sub == 0) else dst
        return remote(src, dst, zs.at[d, sub, t], zr.at[d, sub, t], z_peer[d])

    def y_copy(d, sub, t):
        part = core if sub == 0 else 1 - core
        block = lax.rem(y - t + NY, NY) if d == 0 else lax.rem(y + t, NY)
        dst = gathered[2 + d].at[block, part]
        src = sources[2 + d].at[:, :, own] if (t == 0 and sub == 0) else dst
        return remote(src, dst, ys.at[d, sub, t], yr.at[d, sub, t], y_peer[d])

    sibling = [
        remote(sources[a].at[:, :, other], gathered[a].at[at[a], core], sib_s.at[a], sib_r.at[a], sib)
        for a in range(4)
    ]
    local = [
        pltpu.make_async_copy(sources[a].at[:, :, own], gathered[a].at[at[a], core], loc.at[a])
        for a in range(4)
    ]
    for d in range(2):
        z_copy(d, 0, 0).start()
    for d in range(2):
        y_copy(d, 0, 0).start()
    for copy in sibling:
        copy.start()
    for copy in local:
        copy.start()
    for d in range(2):
        sibling[d].wait_recv()
        z_copy(d, 1, 0).start()
    for d in range(2):
        sibling[2 + d].wait_recv()
        y_copy(d, 1, 0).start()

    def z_step(t):
        for sub in range(2):
            for d in range(2):
                z_copy(d, sub, t - 1).wait_recv()
                if t < NZ - 1:
                    z_copy(d, sub, t).start()

    def y_step(t):
        for sub in range(2):
            for d in range(2):
                y_copy(d, sub, t - 1).wait_recv()
                if t < NY - 1:
                    y_copy(d, sub, t).start()

    z_step(1)
    z_step(2)
    y_step(1)
    z_step(3)
    z_step(4)
    y_step(2)
    z_step(5)
    z_step(6)
    y_step(3)
    z_step(7)
    for copy in local:
        copy.wait()
    for copy in sibling:
        copy.wait_send()
    for d in range(2):
        for sub in range(2):
            for t in range(NZ - 1):
                z_copy(d, sub, t).wait_send()
            for t in range(NY - 1):
                y_copy(d, sub, t).wait_send()


def gather(q, g, k, v):
    return pl.pallas_call(
        gather_kernel,
        out_shape=(
            jax.ShapeDtypeStruct((NZ, NC, CH, SPAN, HALF), bf16),
            jax.ShapeDtypeStruct((NZ, NC, CH, SPAN, HALF), bf16),
            jax.ShapeDtypeStruct((NY, NC, ROWS, NLEN, HALF), bf16),
            jax.ShapeDtypeStruct((NY, NC, ROWS, NLEN, HALF), bf16),
        ),
        in_specs=[ANY] * 4,
        out_specs=(ANY,) * 4,
        scratch_shapes=[
            pltpu.SemaphoreType.DMA((4,)),
            pltpu.SemaphoreType.DMA((4,)),
            pltpu.SemaphoreType.DMA((4,)),
            pltpu.SemaphoreType.DMA((2, 2, NZ - 1)),
            pltpu.SemaphoreType.DMA((2, 2, NZ - 1)),
            pltpu.SemaphoreType.DMA((2, 2, NY - 1)),
            pltpu.SemaphoreType.DMA((2, 2, NY - 1)),
        ],
        compiler_params=pltpu.CompilerParams(collective_id=0, has_side_effects=True),
        name="gather_blocks",
    )(q, g, k, v)


def diagonal(ref, span, pair):
    both = ref[span, :, pl.ds(pair * PAIR, PAIR)]
    blank = jnp.zeros((SPAN, HEAD), both.dtype)
    return jnp.concatenate([
        jnp.concatenate([both[:, :HEAD], blank], axis=1),
        jnp.concatenate([blank, both[:, HEAD:]], axis=1),
    ], axis=0)


def dot(a, b, dims):
    return lax.dot_general(a, b, (dims, ((), ())), preferred_element_type=f32)


NT = ((1,), (1,))
NN = ((1,), (0,))
TN = ((0,), (0,))


def stats_kernel(near, q, g, k, v, stat, count, members):
    row = pl.program_id(0)

    @pl.when(row == 0)
    def _():
        _, z, _ = place()
        for n in range(ROWS_HERE):
            count[n] = 0

        def sort_in(item, carry):
            r = near[item]

            @pl.when(lax.rem(r // (ROWS * NC), NZ) == z)
            def _():
                slot = (r // (ROWS * NC * NZ)) * (NC * ROWS) + lax.rem(r, NC * ROWS)
                filled = count[slot]
                members[slot * SOURCES + filled] = item // NBR
                count[slot] = filled + 1

            return carry

        lax.fori_loop(0, SPANS_HERE * NBR, sort_in, 0)
        stat[:, 0] = jnp.full(stat.shape[:1] + stat.shape[2:], LOWEST, f32)
        stat[:, 1] = jnp.zeros(stat.shape[:1] + stat.shape[2:], f32)

    def item(i, carry):
        span = members[row * SOURCES + i]
        source = span // (NC * CH)
        local = lax.rem(span, NC * CH)
        tops, crosses = [], []
        for pair in range(PAIRS):
            columns = pl.ds(pair * PAIR, PAIR)
            scores = dot(k[0, :, columns], diagonal(q, span, pair), NT) * SCALE
            grad_p = dot(v[0, :, columns], diagonal(g, span, pair), NT)
            highest = jnp.max(scores, axis=0, keepdims=True)
            expons = jnp.exp(scores - highest)
            total = jnp.sum(expons, axis=0, keepdims=True)
            cross = jnp.sum(expons * grad_p, axis=0, keepdims=True)
            tops.append(highest + jnp.log(total))
            crosses.append(cross / total)
        top = jnp.concatenate(tops, axis=0)
        cross = jnp.concatenate(crosses, axis=0)
        old_top = stat[source, 0, local]
        old_cross = stat[source, 1, local]
        peak = jnp.maximum(top, old_top)
        new_w, old_w = jnp.exp(top - peak), jnp.exp(old_top - peak)
        both = new_w + old_w
        stat[source, 0, local] = peak + jnp.log(both)
        stat[source, 1, local] = (new_w * cross + old_w * old_cross) / both
        return carry

    lax.fori_loop(0, count[row], item, 0)


def whole(shape, **more):
    return pl.BlockSpec(shape, lambda *_: (0,) * len(shape), **more)


SMEM = pl.BlockSpec(memory_space=pltpu.SMEM)
ROW_BLOCK = pl.BlockSpec((1, NLEN, HALF), lambda r, *_: (r, 0, 0))
SPAN_BLOCK = whole((SPANS_HERE, SPAN, HALF), pipeline_mode=pl.Buffered(1))
STAT_SHAPE = (NZ, 2, NC * CH, PAIRS, HEAD)


def stats(near, qa, ga, ka, va):
    return pl.pallas_call(
        stats_kernel,
        grid=(ROWS_HERE,),
        out_shape=(
            jax.ShapeDtypeStruct(STAT_SHAPE, f32),
            jax.ShapeDtypeStruct((ROWS_HERE,), jnp.int32),
            jax.ShapeDtypeStruct((ROWS_HERE * SOURCES,), jnp.int32),
        ),
        in_specs=[SMEM, SPAN_BLOCK, SPAN_BLOCK, ROW_BLOCK, ROW_BLOCK],
        out_specs=(whole(STAT_SHAPE), SMEM, SMEM),
        compiler_params=pltpu.CompilerParams(vmem_limit_bytes=48 * 2**20),
        name="part_stats",
    )(near, qa, ga, ka, va)


def combine_kernel(part, full, came, send, recv, send_b, recv_b):
    y, z, core = place()
    peers = [index_of(y, z + s, core) for s in range(1, NZ)]
    greet(peers)
    out = [
        remote(part.at[lax.rem(z + s, NZ)], came.at[z], send.at[s - 1], recv.at[s - 1], peers[s - 1])
        for s in range(1, NZ)
    ]
    for copy in out:
        copy.start()
    came[z] = part[z]
    for copy in out:
        copy.wait_recv()
    tops, crosses = came[:, 0], came[:, 1]
    peak = jnp.max(tops, axis=0)
    weight = jnp.exp(tops - peak[None])
    total = jnp.sum(weight, axis=0)
    full[z, 0] = peak + jnp.log(total)
    full[z, 1] = jnp.sum(weight * crosses, axis=0) / total
    back = [
        remote(full.at[z], full.at[z], send_b.at[s - 1], recv_b.at[s - 1], peers[s - 1])
        for s in range(1, NZ)
    ]
    for copy in back:
        copy.start()
    for copy in back:
        copy.wait_recv()
    for copy in out + back:
        copy.wait_send()


def combine(part):
    vmem = pl.BlockSpec(memory_space=pltpu.VMEM)
    return pl.pallas_call(
        combine_kernel,
        out_shape=jax.ShapeDtypeStruct(STAT_SHAPE, f32),
        in_specs=[vmem],
        out_specs=vmem,
        scratch_shapes=[pltpu.VMEM(STAT_SHAPE, f32)] + [pltpu.SemaphoreType.DMA((NZ - 1,))] * 4,
        compiler_params=pltpu.CompilerParams(collective_id=1, has_side_effects=True),
        name="combine_stats",
    )(part)


def grads_kernel(count, members, q, g, k, v, stat, dq, dk, dv, dk_acc, dv_acc):
    row = pl.program_id(0)

    @pl.when(row == 0)
    def _():
        def clear(n, carry):
            dq[n] = jnp.zeros((SPAN, HALF), bf16)
            return carry

        lax.fori_loop(0, SPANS_HERE, clear, 0)

    dk_acc[...] = jnp.zeros_like(dk_acc)
    dv_acc[...] = jnp.zeros_like(dv_acc)

    def item(i, carry):
        span = members[row * SOURCES + i]
        source = span // (NC * CH)
        local = lax.rem(span, NC * CH)
        log_total = stat[source, 0, local]
        delta = stat[source, 1, local]
        for pair in range(PAIRS):
            columns = pl.ds(pair * PAIR, PAIR)
            keys, values = k[0, :, columns], v[0, :, columns]
            queries, grads = diagonal(q, span, pair), diagonal(g, span, pair)
            scores = dot(keys, queries, NT) * SCALE
            probs = jnp.exp(scores - log_total[pair:pair + 1])
            grad_p = dot(values, grads, NT)
            grad_s = (probs * (grad_p - delta[pair:pair + 1]) * SCALE).astype(bf16)
            dv_acc[:, columns] += dot(probs.astype(bf16), grads, NN)
            dk_acc[:, columns] += dot(grad_s, queries, NN)
            part = dot(grad_s, keys, TN)
            part = jnp.concatenate([part[:SPAN, :HEAD], part[SPAN:, HEAD:]], axis=1)
            part = part.astype(bf16).astype(f32)
            dq[span, :, columns] = (dq[span, :, columns].astype(f32) + part).astype(bf16)
        return carry

    lax.fori_loop(0, count[row], item, 0)
    dk[0] = dk_acc[...].astype(bf16)
    dv[0] = dv_acc[...].astype(bf16)


def grads(count, members, qa, ga, ka, va, stat):
    return pl.pallas_call(
        grads_kernel,
        grid=(ROWS_HERE,),
        out_shape=(
            jax.ShapeDtypeStruct((SPANS_HERE, SPAN, HALF), bf16),
            jax.ShapeDtypeStruct((ROWS_HERE, NLEN, HALF), bf16),
            jax.ShapeDtypeStruct((ROWS_HERE, NLEN, HALF), bf16),
        ),
        in_specs=[SMEM, SMEM, SPAN_BLOCK, SPAN_BLOCK, ROW_BLOCK, ROW_BLOCK, whole(STAT_SHAPE)],
        out_specs=(whole((SPANS_HERE, SPAN, HALF)), ROW_BLOCK, ROW_BLOCK),
        scratch_shapes=[pltpu.VMEM((NLEN, HALF), f32)] * 2,
        compiler_params=pltpu.CompilerParams(vmem_limit_bytes=56 * 2**20),
        name="part_grads",
    )(count, members, qa, ga, ka, va, stat)


def reduce_kernel(dqp, dkp, dvp, dq, dk, dv, z_in, z_own, y_in, y_own,
                  zl, yl, zs, zr, ys, yr, out_s, out_r, out_l):
    y, z, core = place()
    sib = index_of(y, z, 1 - core)
    z_peer = (index_of(y, z + 1, core), index_of(y, z - 1, core))
    y_peer = (index_of(y + 1, z, core), index_of(y - 1, z, core))
    greet((sib,) + z_peer + y_peer)
    own = pl.ds(pl.multiple_of(core * HALF, HALF), HALF)
    y_src = (dkp, dvp)
    side = (1 - core, core)

    def z_block(d, t):
        return lax.rem(z - 1 - t + 2 * NZ, NZ) if d == 0 else lax.rem(z + 1 + t, NZ)

    def y_block(d, t):
        return lax.rem(y - 1 - t + 2 * NY, NY) if d == 0 else lax.rem(y + 1 + t, NY)

    def z_copy(d, t):
        src = dqp.at[z_block(d, 0), side[d]] if t == 0 else z_in.at[d, t - 1]
        return remote(src, z_in.at[d, t], zs.at[d, t], zr.at[d, t], z_peer[d])

    def y_copy(d, sub, t):
        src = y_src[d].at[y_block(d, 0), side[sub]] if t == 0 else y_in.at[d, sub, t - 1]
        return remote(src, y_in.at[d, sub, t], ys.at[d, sub, t], yr.at[d, sub, t], y_peer[d])

    def z_load(d, t):
        return pltpu.make_async_copy(dqp.at[z_block(d, t + 1), side[d]], z_own.at[d, t], zl.at[d, t])

    def y_load(d, sub, t):
        return pltpu.make_async_copy(
            y_src[d].at[y_block(d, t + 1), side[sub]], y_own.at[d, sub, t], yl.at[d, sub, t])

    for d in range(2):
        y_copy(d, 0, 0).start()
    for d in range(2):
        z_copy(d, 0).start()
    for d in range(2):
        y_copy(d, 1, 0).start()
    for t in range(NY - 1):
        for sub in range(2):
            for d in range(2):
                y_load(d, sub, t).start()
    for t in range(NZ - 1):
        for d in range(2):
            z_load(d, t).start()

    def add(total, more, count):
        def one(n, carry):
            total[n] = (total[n].astype(f32) + more[n].astype(f32)).astype(bf16)
            return carry

        lax.fori_loop(0, count, one, 0)

    def finish(which, out, src):
        there = remote(src[0], out.at[:, :, own], out_s.at[which], out_r.at[which], sib)
        here = pltpu.make_async_copy(src[1], out.at[:, :, own], out_l.at[which])
        return there, here

    ends = (
        finish(0, dk, (y_in.at[0, 0, NY - 2], y_in.at[0, 1, NY - 2])),
        finish(1, dv, (y_in.at[1, 0, NY - 2], y_in.at[1, 1, NY - 2])),
        finish(2, dq, (z_in.at[0, NZ - 2], z_in.at[1, NZ - 2])),
    )

    def z_step(t):
        for d in range(2):
            z_copy(d, t).wait_recv()
            z_load(d, t).wait()
            add(z_in.at[d, t], z_own.at[d, t], CH)
            if t < NZ - 2:
                z_copy(d, t + 1).start()
            else:
                ends[2][d].start()

    def y_step(t, sub):
        for d in range(2):
            y_copy(d, sub, t).wait_recv()
            y_load(d, sub, t).wait()
            add(y_in.at[d, sub, t], y_own.at[d, sub, t], ROWS)
            if t < NY - 2:
                y_copy(d, sub, t + 1).start()
            else:
                ends[d][sub].start()

    z_step(0)
    y_step(0, 0)
    z_step(1)
    y_step(0, 1)
    z_step(2)
    y_step(1, 0)
    z_step(3)
    z_step(4)
    y_step(1, 1)
    z_step(5)
    y_step(2, 0)
    z_step(6)
    y_step(2, 1)
    for there, here in ends:
        there.wait()
        here.wait()
    for d in range(2):
        for t in range(NZ - 1):
            z_copy(d, t).wait_send()
        for sub in range(2):
            for t in range(NY - 1):
                y_copy(d, sub, t).wait_send()


def reduce(dqp, dkp, dvp):
    sem = pltpu.SemaphoreType.DMA
    return pl.pallas_call(
        reduce_kernel,
        out_shape=(
            jax.ShapeDtypeStruct((CH, SPAN, WIDE), bf16),
            jax.ShapeDtypeStruct((ROWS, NLEN, WIDE), bf16),
            jax.ShapeDtypeStruct((ROWS, NLEN, WIDE), bf16),
        ),
        in_specs=[ANY] * 3,
        out_specs=(ANY,) * 3,
        scratch_shapes=[
            pltpu.VMEM((2, NZ - 1, CH, SPAN, HALF), bf16),
            pltpu.VMEM((2, NZ - 1, CH, SPAN, HALF), bf16),
            pltpu.VMEM((2, 2, NY - 1, ROWS, NLEN, HALF), bf16),
            pltpu.VMEM((2, 2, NY - 1, ROWS, NLEN, HALF), bf16),
            sem((2, NZ - 1)),
            sem((2, 2, NY - 1)),
            sem((2, NZ - 1)),
            sem((2, NZ - 1)),
            sem((2, 2, NY - 1)),
            sem((2, 2, NY - 1)),
            sem((3,)),
            sem((3,)),
            sem((3,)),
        ],
        compiler_params=pltpu.CompilerParams(
            collective_id=2, has_side_effects=True, vmem_limit_bytes=56 * 2**20),
        name="reduce_blocks",
    )(dqp, dkp, dvp)


def per_device(queries, out_grad, row_keys, row_values, neighbours):
    y, _, _ = place()
    lists = lax.all_gather(neighbours, ("seq", "mp"), axis=0, tiled=True)
    near = lax.dynamic_slice_in_dim(lists, y * SPANS_HERE, SPANS_HERE, 0).reshape(-1)
    qa, ga, ka, va = gather(queries, out_grad, row_keys, row_values)
    qa = qa.reshape(SPANS_HERE, SPAN, HALF)
    ga = ga.reshape(SPANS_HERE, SPAN, HALF)
    ka = ka.reshape(ROWS_HERE, NLEN, HALF)
    va = va.reshape(ROWS_HERE, NLEN, HALF)
    part, count, members = stats(near, qa, ga, ka, va)
    full = combine(part)
    dqp, dkp, dvp = grads(count, members, qa, ga, ka, va, full)
    return reduce(
        dqp.reshape(NZ, NC, CH, SPAN, HALF),
        dkp.reshape(NY, NC, ROWS, NLEN, HALF),
        dvp.reshape(NY, NC, ROWS, NLEN, HALF),
    )


def solution(mesh):
    in_specs = (
        P("seq", None, "mp"),
        P("seq", None, "mp"),
        P("seq", None, "mp"),
        P("seq", None, "mp"),
        P(("seq", "mp"), None),
    )
    out_specs = (P("seq", None, "mp"), P("seq", None, "mp"), P("seq", None, "mp"))
    return jax.shard_map(
        per_device, mesh=mesh, in_specs=in_specs, out_specs=out_specs, check_vma=False
    )
```

time: 1280 us -> 565 us (0.44)
  waiting for transfers between devices: 586 us -> 0 us
  Pallas kernels: 0 us -> 445 us
  local copies, waits for them, and re-layouts: 331 us -> 10.4 us
  other arithmetic: 161 us -> 0 us
  matrix products: 120 us -> 0 us
  blocking collectives: 8.91 us -> 107 us
  starting transfers between devices: 69.2 us -> 0 us
    all_to_all x9 -> x0, waiting for transfers between devices: 586 us -> none  [the longest x1 184 us: per_device(): lax.all_to_all(grad_send, 'seq', split_axis=0, concat_axis=0, tiled=True)]
    pallas_call x0 -> x5, Pallas kernels: none -> 445 us  [the longest x1 164 us: gather(): pl.pallas_call(gather_kernel, out_shape=(jax.ShapeDtypeStruct((NZ, NC, CH...]
    scatter-add x16 -> x0, other arithmetic: 141 us -> none  [the longest x8 71.1 us: second_pass(): key_acc.at[row_block].add(key_part)]
    dot_general x56 -> x0, matrix products: 120 us -> none  [the longest x8 36.2 us: second_pass(): jnp.einsum('bhij,bihd->bjhd', probs_low, grad_heads, preferred_element_ty...]
    gather x38 -> x0, local copies, waits for them, and re-layouts: 101 us -> none  [the longest x8 28.8 us: first_pass(): value_heads = split_heads(row_values[row_block])]
    all_gather x1, blocking collectives: 8.91 us -> 107 us  [per_device(): lists = lax.all_gather(neighbours, ('seq', 'mp'), axis=0, tiled=True)]
    reshape x22 -> x1, local copies, waits for them, and re-layouts: 86.5 us -> 0.14 us  [per_device(): lax.dynamic_slice_in_dim(lists, y * SPANS_HERE, SPANS_HERE, 0).reshape(-1)]
    all_to_all x9 -> x0, starting transfers between devices: 69.2 us -> none  [the longest x1 14.3 us: per_device(): lax.all_to_all(row_send, 'seq', split_axis=0, concat_axis=0, tiled=True)]
  transfers between devices with their start and end apart: 9 -> 0, of which waited for: 8 -> 0; matrix products, arithmetic and copies ran while one was open for 2% -> 0% of each run, Pallas kernels for 0% -> 0%
where the time goes in v1:
time: 565 us; the launch traced here: 563 us
  Pallas kernels  445 us (79%)
  blocking collectives  107 us (19%)
  local copies, waits for them, and re-layouts  10.4 us (2%)
    pallas_call x1, Pallas kernels, gather(): pl.pallas_call(gather_kernel, out_shape=(jax.ShapeDtypeStruct((NZ, NC, CH...  164 us
    pallas_call x1, Pallas kernels, reduce(): pl.pallas_call(reduce_kernel, out_shape=(jax.ShapeDtypeStruct((CH, SPAN,...  149 us
    all_gather x1, blocking collectives, per_device(): lists = lax.all_gather(neighbours, ('seq', 'mp'), axis=0, tiled=True)  107 us
    pallas_call x1, Pallas kernels, grads(): pl.pallas_call(grads_kernel, grid=(ROWS_HERE,), out_shape=(jax.ShapeDtype...  60.7 us
    pallas_call x1, Pallas kernels, stats(): pl.pallas_call(stats_kernel, grid=(ROWS_HERE,), out_shape=(jax.ShapeDtype...  49.7 us
    pallas_call x1, Pallas kernels, combine(): pl.pallas_call(combine_kernel, out_shape=jax.ShapeDtypeStruct(STAT_SHAPE,...  21.8 us

profile of v1, /device:TPU:1, one launch (start us, length us, event | category | flops | bytes accessed | tf_op | source)
XLA Modules:
  0.0 563.1 jit_solution(17909244084034720385)
XLA Ops:
  0.6 107.0 %all-gather = s32[256,2,2]{2,1,0:T(2,128)S(1)} all-gather(s32[1,2,2]{2,1,0:T(2,128)} %bitcast.21), channel_id=1, replica_groups=mesh['seq'=64,'mp'=4] {'seq','mp'}, dimensions={0}, use_global_device_ids=true | all-gather | bytes 4112 | tf_op jit(solution)/shard_map/all_gather | solution.py:507
  107.6 0.1 reshape.30.near
  107.8 163.8 %gather_blocks.1 = (bf16[8,2,8,64,512]{4,3,2,1,0:T(8,128)(2,1)}, bf16[8,2,8,64,512]{4,3,2,1,0:T(8,128)(2,1)}, bf16[4,2,8,128,512]{4,3,2,1,0:T(8,128)(2,1)}, bf16[4,2,8,128,512]{4,3,2,1,0:T(8,128)(2,1)}) custom-call(bf16[8,64,1024]{2,1,0:T(8,128)(2,1)} %q.1, bf16[8,64,1024]{2,1,0:T(8,128)(2,1)} %g.1, bf16[8,128,1024]{2,1,0:T(8,128)(2,1)} %k.1, ...), custom_call_target="tpu_custom_call" | custom-call | tf_op jit(solution)/shard_map/gather_blocks/pallas_call | solution.py:141
  271.6 49.7 %part_stats.1 = (f32[8,2,16,2,128]{4,3,2,1,0:T(2,128)S(1)}, s32[64]{0:T(128)S(1)}, s32[1024]{0:T(1024)S(1)}) custom-call(s32[256]{0:T(256)S(1)} %reshape.30.near, bf16[128,64,512]{2,1,0:T(8,128)(2,1)} %bitcast.9, bf16[128,64,512]{2,1,0:T(8,128)(2,1)} %bitcast.11, bf16[64,128,512]{2,1,0:T(8,128)(2,1)} %bitcast.13, bf16[64,128,512]{2,1,0:T(8,128)(2,1)} %bitcast.15), custom_call_target="tpu_custom_call" | custom-call | tf_op jit(solution)/shard_map/part_stats/pallas_call | solution.py:248
  321.4 0.0 copy-start
  321.4 0.7 copy-done
  322.1 0.0 copy-start.1
  322.1 0.6 copy-done.1
  322.7 0.0 copy-start.2
  322.7 0.5 copy-done.2
  323.2 21.8 %combine_stats.1.stat = f32[8,2,16,2,128]{4,3,2,1,0:T(2,128)} custom-call(f32[8,2,16,2,128]{4,3,2,1,0:T(2,128)} %copy-done), custom_call_target="tpu_custom_call" | custom-call | tf_op jit(solution)/shard_map/combine_stats/pallas_call | solution.py:296
  345.0 60.7 %part_grads.1 = (bf16[128,64,512]{2,1,0:T(8,128)(2,1)}, bf16[64,128,512]{2,1,0:T(8,128)(2,1)}, bf16[64,128,512]{2,1,0:T(8,128)(2,1)}) custom-call(s32[64]{0:T(128)} %copy-done.2, s32[1024]{0:T(1024)} %copy-done.1, bf16[128,64,512]{2,1,0:T(8,128)(2,1)} %bitcast.10, bf16[128,64,512]{2,1,0:T(8,128)(2,1)} %bitcast.12, bf16[64,128,512]{2,1,0:T(8,128)(2,1)} %bitcast.14, ...), custom_call_target="tpu_custom_call" | custom-call | tf_op jit(solution)/shard_map/part_grads/pallas_call | solution.py:349
  405.7 148.9 %reduce_blocks.1 = (bf16[8,64,1024]{2,1,0:T(8,128)(2,1)}, bf16[8,128,1024]{2,1,0:T(8,128)(2,1)}, bf16[8,128,1024]{2,1,0:T(8,128)(2,1)}) custom-call(bf16[8,2,8,64,512]{4,3,2,1,0:T(8,128)(2,1)} %bitcast.17, bf16[4,2,8,128,512]{4,3,2,1,0:T(8,128)(2,1)} %bitcast.18, bf16[4,2,8,128,512]{4,3,2,1,0:T(8,128)(2,1)} %bitcast.19), custom_call_target="tpu_custom_call" | custom-call | tf_op jit(solution)/shard_map/reduce_blocks/pallas_call | solution.py:475
  554.6 2.3 copy.11
  556.9 3.1 copy.12
  560.0 3.1 copy.13
  (1 shorter events, 0.0 us)
Async XLA Ops:
  321.4 0.7 copy-start
  322.1 0.6 copy-start.1
  322.7 0.5 copy-start.2

commit v2 on v1

--- a/solution.py
+++ b/solution.py
@@ -11,7 +11,7 @@
 SPAN = 64
 NLEN = 128
 NBR = 2
-NY, NZ, NC = 4, 8, 2
+NX, NY, NZ, NC = 4, 4, 8, 2
 CH, ROWS = 8, 8
 WIDE = 1024
 HALF = WIDE // NC
@@ -19,7 +19,8 @@
 PAIRS = HALF // PAIR
 SOURCES = NZ * NC
 SPANS_HERE = SOURCES * CH
-ROWS_HERE = NY * NC * ROWS
+OWNERS_HERE = NY * NC
+ROWS_HERE = OWNERS_HERE * ROWS
 SCALE = HEAD ** (-0.5)
 LOWEST = -1e30
 MESH = pl.DeviceIdType.MESH
@@ -52,12 +53,33 @@
         device_id={"seq": peer}, device_id_type=MESH)
 
 
-def gather_kernel(q, g, k, v, qa, ga, ka, va, loc, sib_s, sib_r, zs, zr, ys, yr):
+def gather_kernel(q, g, k, v, lists, qa, ga, ka, va, near, loc, sib_s, sib_r, zs, zr, ys, yr,
+                  near_s, near_r):
     y, z, core = place()
+    mp = lax.axis_index("mp")
     sib = index_of(y, z, 1 - core)
     z_peer = (index_of(y, z + 1, core), index_of(y, z - 1, core))
     y_peer = (index_of(y + 1, z, core), index_of(y - 1, z, core))
-    greet((sib,) + z_peer + y_peer)
+    line = [index_of(y, z + s, core) for s in range(1, NZ)]
+    line += [index_of(y, z + s, 1 - core) for s in range(NZ)]
+    barrier = pltpu.get_barrier_semaphore()
+    for s in range(1, NX):
+        pl.semaphore_signal(
+            barrier, inc=1, device_id={"mp": lax.rem(mp + s, NX)}, device_id_type=MESH)
+    for peer in line + list(y_peer):
+        pl.semaphore_signal(barrier, inc=1, device_id={"seq": peer}, device_id_type=MESH)
+    pl.semaphore_wait(barrier, NX - 1 + len(line) + len(y_peer))
+    mine = z * NC + core
+    near_x = [
+        pltpu.make_async_remote_copy(
+            src_ref=lists, dst_ref=near.at[mine, mp], send_sem=near_s.at[s - 1],
+            recv_sem=near_r.at[s - 1], device_id={"mp": lax.rem(mp + s, NX)}, device_id_type=MESH)
+        for s in range(1, NX)
+    ]
+    near_line = [
+        remote(near.at[mine], near.at[mine], near_s.at[NX - 1 + n], near_r.at[NX - 1 + n], peer)
+        for n, peer in enumerate(line)
+    ]
     own = pl.ds(pl.multiple_of(core * HALF, HALF), HALF)
     other = pl.ds(pl.multiple_of((1 - core) * HALF, HALF), HALF)
     sources = (q, g, k, v)
@@ -92,14 +114,22 @@
         y_copy(d, 0, 0).start()
     for copy in sibling:
         copy.start()
+    for copy in near_x:
+        copy.start()
     for copy in local:
         copy.start()
+    near[mine, mp] = lists[...]
     for d in range(2):
         sibling[d].wait_recv()
         z_copy(d, 1, 0).start()
     for d in range(2):
         sibling[2 + d].wait_recv()
         y_copy(d, 1, 0).start()
+
+    for copy in near_x:
+        copy.wait_recv()
+    for copy in near_line:
+        copy.start()
 
     def z_step(t):
         for sub in range(2):
@@ -125,6 +155,10 @@
     z_step(6)
     y_step(3)
     z_step(7)
+    for copy in near_line:
+        copy.wait_recv()
+    for copy in near_x + near_line:
+        copy.wait_send()
     for copy in local:
         copy.wait()
     for copy in sibling:
@@ -137,7 +171,9 @@
                 y_copy(d, sub, t).wait_send()
 
 
-def gather(q, g, k, v):
+def gather(q, g, k, v, lists):
+    sem = pltpu.SemaphoreType.DMA
+    vmem = pl.BlockSpec(memory_space=pltpu.VMEM)
     return pl.pallas_call(
         gather_kernel,
         out_shape=(
@@ -145,21 +181,24 @@
             jax.ShapeDtypeStruct((NZ, NC, CH, SPAN, HALF), bf16),
             jax.ShapeDtypeStruct((NY, NC, ROWS, NLEN, HALF), bf16),
             jax.ShapeDtypeStruct((NY, NC, ROWS, NLEN, HALF), bf16),
+            jax.ShapeDtypeStruct((SOURCES, NX, 1, 128), jnp.int32),
         ),
-        in_specs=[ANY] * 4,
-        out_specs=(ANY,) * 4,
+        in_specs=[ANY] * 4 + [vmem],
+        out_specs=(ANY,) * 4 + (vmem,),
         scratch_shapes=[
-            pltpu.SemaphoreType.DMA((4,)),
-            pltpu.SemaphoreType.DMA((4,)),
-            pltpu.SemaphoreType.DMA((4,)),
-            pltpu.SemaphoreType.DMA((2, 2, NZ - 1)),
-            pltpu.SemaphoreType.DMA((2, 2, NZ - 1)),
-            pltpu.SemaphoreType.DMA((2, 2, NY - 1)),
-            pltpu.SemaphoreType.DMA((2, 2, NY - 1)),
+            sem((4,)),
+            sem((4,)),
+            sem((4,)),
+            sem((2, 2, NZ - 1)),
+            sem((2, 2, NZ - 1)),
+            sem((2, 2, NY - 1)),
+            sem((2, 2, NY - 1)),
+            sem((NX - 1 + SOURCES - 1,)),
+            sem((NX - 1 + SOURCES - 1,)),
         ],
         compiler_params=pltpu.CompilerParams(collective_id=0, has_side_effects=True),
         name="gather_blocks",
-    )(q, g, k, v)
+    )(q, g, k, v, lists)
 
 
 def diagonal(ref, span, pair):
@@ -181,12 +220,12 @@
 
 
 def stats_kernel(near, q, g, k, v, stat, count, members):
-    row = pl.program_id(0)
-
-    @pl.when(row == 0)
+    owner = pl.program_id(0)
+
+    @pl.when(owner == 0)
     def _():
         _, z, _ = place()
-        for n in range(ROWS_HERE):
+        for n in range(OWNERS_HERE):
             count[n] = 0
 
         def sort_in(item, carry):
@@ -194,9 +233,9 @@
 
             @pl.when(lax.rem(r // (ROWS * NC), NZ) == z)
             def _():
-                slot = (r // (ROWS * NC * NZ)) * (NC * ROWS) + lax.rem(r, NC * ROWS)
+                slot = (r // (ROWS * NC * NZ)) * NC + lax.rem(r // ROWS, NC)
                 filled = count[slot]
-                members[slot * SOURCES + filled] = item // NBR
+                members[slot * SOURCES + filled] = (item // NBR) * ROWS + lax.rem(r, ROWS)
                 count[slot] = filled + 1
 
             return carry
@@ -206,14 +245,15 @@
         stat[:, 1] = jnp.zeros(stat.shape[:1] + stat.shape[2:], f32)
 
     def item(i, carry):
-        span = members[row * SOURCES + i]
+        member = members[owner * SOURCES + i]
+        span, row = member // ROWS, lax.rem(member, ROWS)
         source = span // (NC * CH)
         local = lax.rem(span, NC * CH)
         tops, crosses = [], []
         for pair in range(PAIRS):
             columns = pl.ds(pair * PAIR, PAIR)
-            scores = dot(k[0, :, columns], diagonal(q, span, pair), NT) * SCALE
-            grad_p = dot(v[0, :, columns], diagonal(g, span, pair), NT)
+            scores = dot(k[row, :, columns], diagonal(q, span, pair), NT) * SCALE
+            grad_p = dot(v[row, :, columns], diagonal(g, span, pair), NT)
             highest = jnp.max(scores, axis=0, keepdims=True)
             expons = jnp.exp(scores - highest)
             total = jnp.sum(expons, axis=0, keepdims=True)
@@ -231,7 +271,7 @@
         stat[source, 1, local] = (new_w * cross + old_w * old_cross) / both
         return carry
 
-    lax.fori_loop(0, count[row], item, 0)
+    lax.fori_loop(0, count[owner], item, 0)
 
 
 def whole(shape, **more):
@@ -239,7 +279,7 @@
 
 
 SMEM = pl.BlockSpec(memory_space=pltpu.SMEM)
-ROW_BLOCK = pl.BlockSpec((1, NLEN, HALF), lambda r, *_: (r, 0, 0))
+ROW_BLOCK = pl.BlockSpec((ROWS, NLEN, HALF), lambda n: (n, 0, 0))
 SPAN_BLOCK = whole((SPANS_HERE, SPAN, HALF), pipeline_mode=pl.Buffered(1))
 STAT_SHAPE = (NZ, 2, NC * CH, PAIRS, HEAD)
 
@@ -247,11 +287,11 @@
 def stats(near, qa, ga, ka, va):
     return pl.pallas_call(
         stats_kernel,
-        grid=(ROWS_HERE,),
+        grid=(OWNERS_HERE,),
         out_shape=(
             jax.ShapeDtypeStruct(STAT_SHAPE, f32),
-            jax.ShapeDtypeStruct((ROWS_HERE,), jnp.int32),
-            jax.ShapeDtypeStruct((ROWS_HERE * SOURCES,), jnp.int32),
+            jax.ShapeDtypeStruct((OWNERS_HERE,), jnp.int32),
+            jax.ShapeDtypeStruct((OWNERS_HERE * SOURCES,), jnp.int32),
         ),
         in_specs=[SMEM, SPAN_BLOCK, SPAN_BLOCK, ROW_BLOCK, ROW_BLOCK],
         out_specs=(whole(STAT_SHAPE), SMEM, SMEM),
@@ -305,9 +345,9 @@
 
 
 def grads_kernel(count, members, q, g, k, v, stat, dq, dk, dv, dk_acc, dv_acc):
-    row = pl.program_id(0)
-
-    @pl.when(row == 0)
+    owner = pl.program_id(0)
+
+    @pl.when(owner == 0)
     def _():
         def clear(n, carry):
             dq[n] = jnp.zeros((SPAN, HALF), bf16)
@@ -315,40 +355,50 @@
 
         lax.fori_loop(0, SPANS_HERE, clear, 0)
 
-    dk_acc[...] = jnp.zeros_like(dk_acc)
-    dv_acc[...] = jnp.zeros_like(dv_acc)
+    def fresh(n, carry):
+        dk_acc[n] = jnp.zeros((NLEN, HALF), f32)
+        dv_acc[n] = jnp.zeros((NLEN, HALF), f32)
+        return carry
+
+    lax.fori_loop(0, ROWS, fresh, 0)
 
     def item(i, carry):
-        span = members[row * SOURCES + i]
+        member = members[owner * SOURCES + i]
+        span, row = member // ROWS, lax.rem(member, ROWS)
         source = span // (NC * CH)
         local = lax.rem(span, NC * CH)
         log_total = stat[source, 0, local]
         delta = stat[source, 1, local]
         for pair in range(PAIRS):
             columns = pl.ds(pair * PAIR, PAIR)
-            keys, values = k[0, :, columns], v[0, :, columns]
+            keys, values = k[row, :, columns], v[row, :, columns]
             queries, grads = diagonal(q, span, pair), diagonal(g, span, pair)
             scores = dot(keys, queries, NT) * SCALE
             probs = jnp.exp(scores - log_total[pair:pair + 1])
             grad_p = dot(values, grads, NT)
             grad_s = (probs * (grad_p - delta[pair:pair + 1]) * SCALE).astype(bf16)
-            dv_acc[:, columns] += dot(probs.astype(bf16), grads, NN)
-            dk_acc[:, columns] += dot(grad_s, queries, NN)
+            dv_acc[row, :, columns] += dot(probs.astype(bf16), grads, NN)
+            dk_acc[row, :, columns] += dot(grad_s, queries, NN)
             part = dot(grad_s, keys, TN)
             part = jnp.concatenate([part[:SPAN, :HEAD], part[SPAN:, HEAD:]], axis=1)
             part = part.astype(bf16).astype(f32)
             dq[span, :, columns] = (dq[span, :, columns].astype(f32) + part).astype(bf16)
         return carry
 
-    lax.fori_loop(0, count[row], item, 0)
-    dk[0] = dk_acc[...].astype(bf16)
-    dv[0] = dv_acc[...].astype(bf16)
+    lax.fori_loop(0, count[owner], item, 0)
+
+    def settle(n, carry):
+        dk[n] = dk_acc[n].astype(bf16)
+        dv[n] = dv_acc[n].astype(bf16)
+        return carry
+
+    lax.fori_loop(0, ROWS, settle, 0)
 
 
 def grads(count, members, qa, ga, ka, va, stat):
     return pl.pallas_call(
         grads_kernel,
-        grid=(ROWS_HERE,),
+        grid=(OWNERS_HERE,),
         out_shape=(
             jax.ShapeDtypeStruct((SPANS_HERE, SPAN, HALF), bf16),
             jax.ShapeDtypeStruct((ROWS_HERE, NLEN, HALF), bf16),
@@ -356,7 +406,7 @@
         ),
         in_specs=[SMEM, SMEM, SPAN_BLOCK, SPAN_BLOCK, ROW_BLOCK, ROW_BLOCK, whole(STAT_SHAPE)],
         out_specs=(whole((SPANS_HERE, SPAN, HALF)), ROW_BLOCK, ROW_BLOCK),
-        scratch_shapes=[pltpu.VMEM((NLEN, HALF), f32)] * 2,
+        scratch_shapes=[pltpu.VMEM((ROWS, NLEN, HALF), f32)] * 2,
         compiler_params=pltpu.CompilerParams(vmem_limit_bytes=56 * 2**20),
         name="part_grads",
     )(count, members, qa, ga, ka, va, stat)
@@ -503,10 +553,10 @@
 
 
 def per_device(queries, out_grad, row_keys, row_values, neighbours):
-    y, _, _ = place()
-    lists = lax.all_gather(neighbours, ("seq", "mp"), axis=0, tiled=True)
-    near = lax.dynamic_slice_in_dim(lists, y * SPANS_HERE, SPANS_HERE, 0).reshape(-1)
-    qa, ga, ka, va = gather(queries, out_grad, row_keys, row_values)
+    few = neighbours.size
+    lists = jnp.pad(neighbours.reshape(1, few), ((0, 0), (0, 128 - few)))
+    qa, ga, ka, va, near = gather(queries, out_grad, row_keys, row_values, lists)
+    near = near[:, :, 0, :few].reshape(-1)
     qa = qa.reshape(SPANS_HERE, SPAN, HALF)
     ga = ga.reshape(SPANS_HERE, SPAN, HALF)
     ka = ka.reshape(ROWS_HERE, NLEN, HALF)

time: 565 us -> 427 us (0.76)
  blocking collectives: 107 us -> 0 us
  Pallas kernels: 445 us -> 412 us
    all_gather x1 -> x0, blocking collectives: 107 us -> none  [per_device(): lists = lax.all_gather(neighbours, ('seq', 'mp'), axis=0, tiled=True)]
    pallas_call x2, Pallas kernels: 110 us -> 56.8 us  [the longest x1 33 us: grads(): pl.pallas_call(grads_kernel, grid=(OWNERS_HERE,), out_shape=(jax.ShapeDty...]
    pallas_call x1, Pallas kernels: 149 us -> 157 us  [reduce(): pl.pallas_call(reduce_kernel, out_shape=(jax.ShapeDtypeStruct((CH, SPAN,...]
    pallas_call x1, Pallas kernels: 164 us -> 171 us  [gather(): pl.pallas_call(gather_kernel, out_shape=(jax.ShapeDtypeStruct((NZ, NC, CH...]
where the time goes in v2:
time: 427 us; the launch traced here: 425 us
  Pallas kernels  412 us (96%)
  local copies, waits for them, and re-layouts  12.4 us (3%)
    pallas_call x1, Pallas kernels, gather(): pl.pallas_call(gather_kernel, out_shape=(jax.ShapeDtypeStruct((NZ, NC, CH...  171 us
    pallas_call x1, Pallas kernels, reduce(): pl.pallas_call(reduce_kernel, out_shape=(jax.ShapeDtypeStruct((CH, SPAN,...  157 us
    pallas_call x1, Pallas kernels, grads(): pl.pallas_call(grads_kernel, grid=(OWNERS_HERE,), out_shape=(jax.ShapeDty...  33 us
    pallas_call x1, Pallas kernels, combine(): pl.pallas_call(combine_kernel, out_shape=jax.ShapeDtypeStruct(STAT_SHAPE,...  27.4 us
    pallas_call x1, Pallas kernels, stats(): pl.pallas_call(stats_kernel, grid=(OWNERS_HERE,), out_shape=(jax.ShapeDty...  23.8 us
    unnamed x9, local copies, waits for them, and re-layouts  10.1 us

profile of v2, /device:TPU:1, one launch (start us, length us, event | category | flops | bytes accessed | tf_op | source)
XLA Modules:
  0.0 424.8 jit_solution(12531034355447989033)
XLA Ops:
  0.6 0.8 reshape.30
  1.4 0.5 pad.4.lists
  1.9 170.7 %gather_blocks.1 = (bf16[8,2,8,64,512]{4,3,2,1,0:T(8,128)(2,1)}, bf16[8,2,8,64,512]{4,3,2,1,0:T(8,128)(2,1)}, bf16[4,2,8,128,512]{4,3,2,1,0:T(8,128)(2,1)}, bf16...) custom-call(bf16[8,64,1024]{2,1,0:T(8,128)(2,1)} %q.1, bf16[8,64,1024]{2,1,0:T(8,128)(2,1)} %g.1, ...), custom_call_target="tpu_custom_call" | custom-call | tf_op jit(solution)/shard_map/gather_blocks/pallas_call | solution.py:177
  172.6 0.8 slice_reduce_fusion
  173.5 0.1 reshape_squeeze.3.near
  173.6 23.8 %part_stats.1 = (f32[8,2,16,2,128]{4,3,2,1,0:T(2,128)S(1)}, s32[8]{0:T(128)S(1)}, s32[128]{0:T(128)S(1)}) custom-call(s32[256]{0:T(256)S(1)} %reshape_squeeze.3.near, bf16[128,64,512]{2,1,0:T(8,128)(2,1)} %bitcast.7, bf16[128,64,512]{2,1,0:T(8,128)(2,1)} %bitcast.9, bf16[64,128,512]{2,1,0:T(8,128)(2,1)} %bitcast.11, bf16[64,128,512]{2,1,0:T(8,128)(2,1)} %bitcast.13), custom_call_target="tpu_custom_call" | custom-call | tf_op jit(solution)/shard_map/part_stats/pallas_call | solution.py:288
  197.4 0.0 copy-start
  197.4 0.7 copy-done
  198.1 0.0 copy-start.1
  198.1 0.5 copy-done.1
  198.6 0.0 copy-start.2
  198.6 0.5 copy-done.2
  199.1 27.4 %combine_stats.1.stat = f32[8,2,16,2,128]{4,3,2,1,0:T(2,128)} custom-call(f32[8,2,16,2,128]{4,3,2,1,0:T(2,128)} %copy-done), custom_call_target="tpu_custom_call" | custom-call | tf_op jit(solution)/shard_map/combine_stats/pallas_call | solution.py:336
  226.6 33.0 %part_grads.1 = (bf16[128,64,512]{2,1,0:T(8,128)(2,1)}, bf16[64,128,512]{2,1,0:T(8,128)(2,1)}, bf16[64,128,512]{2,1,0:T(8,128)(2,1)}) custom-call(s32[8]{0:T(128)} %copy-done.1, s32[128]{0:T(128)} %copy-done.2, bf16[128,64,512]{2,1,0:T(8,128)(2,1)} %bitcast.8, bf16[128,64,512]{2,1,0:T(8,128)(2,1)} %bitcast.10, bf16[64,128,512]{2,1,0:T(8,128)(2,1)} %bitcast.12, ...), custom_call_target="tpu_custom_call" | custom-call | tf_op jit(solution)/shard_map/part_grads/pallas_call | solution.py:399
  259.6 156.8 %reduce_blocks.1 = (bf16[8,64,1024]{2,1,0:T(8,128)(2,1)}, bf16[8,128,1024]{2,1,0:T(8,128)(2,1)}, bf16[8,128,1024]{2,1,0:T(8,128)(2,1)}) custom-call(bf16[8,2,8,64,512]{4,3,2,1,0:T(8,128)(2,1)} %bitcast.15, bf16[4,2,8,128,512]{4,3,2,1,0:T(8,128)(2,1)} %bitcast.16, bf16[4,2,8,128,512]{4,3,2,1,0:T(8,128)(2,1)} %bitcast.17), custom_call_target="tpu_custom_call" | custom-call | tf_op jit(solution)/shard_map/reduce_blocks/pallas_call | solution.py:525
  416.4 2.3 copy.11
  418.6 3.1 copy.12
  421.7 3.1 copy.13
Async XLA Ops:
  197.4 0.7 copy-start
  198.1 0.5 copy-start.1
  198.6 0.5 copy-start.2

commit v3 on v2

v3 whole, which is shorter than its diff:
```python
import jax
import jax.numpy as jnp
from jax import lax
from jax.experimental import pallas as pl
from jax.experimental.pallas import tpu as pltpu
from jax.sharding import PartitionSpec as P

HEAD = 128
SPAN = 64
NLEN = 128
NBR = 2
NX, NY, NZ, NC = 4, 4, 8, 2
CH, ROWS = 8, 8
WIDE = 1024
HALF = WIDE // NC
PAIR = 2 * HEAD
PAIRS = HALF // PAIR
SOURCES = NZ * NC
SPANS_HERE = SOURCES * CH
OWNERS_HERE = NY * NC
ROWS_HERE = OWNERS_HERE * ROWS
SCALE = HEAD ** (-0.5)
MESH = pl.DeviceIdType.MESH
ANY = pl.BlockSpec(memory_space=pl.ANY)
f32, bf16 = jnp.float32, jnp.bfloat16


def place():
    me = lax.axis_index("seq")
    core = lax.rem(me, NC)
    z = lax.rem(me // NC, NZ)
    y = me // (NC * NZ)
    return y, z, core


def index_of(y, z, core):
    return (lax.rem(y + NY, NY) * NZ + lax.rem(z + NZ, NZ)) * NC + core


def greet(peers):
    barrier = pltpu.get_barrier_semaphore()
    for peer in peers:
        pl.semaphore_signal(barrier, inc=1, device_id={"seq": peer}, device_id_type=MESH)
    pl.semaphore_wait(barrier, len(peers))


def remote(src, dst, send_sem, recv_sem, peer):
    return pltpu.make_async_remote_copy(
        src_ref=src, dst_ref=dst, send_sem=send_sem, recv_sem=recv_sem,
        device_id={"seq": peer}, device_id_type=MESH)


NT = ((1,), (1,))
NN = ((1,), (0,))
TN = ((0,), (0,))


def dot(a, b, dims):
    return lax.dot_general(a, b, (dims, ((), ())), preferred_element_type=f32)


def diagonal(both):
    blank = jnp.zeros((SPAN, HEAD), both.dtype)
    return jnp.concatenate([
        jnp.concatenate([both[:, :HEAD], blank], axis=1),
        jnp.concatenate([blank, both[:, HEAD:]], axis=1),
    ], axis=0)


def gather_kernel(q, g, k, v, lists, qa, ga, ka, va, table, hits, full,
                  qc, gc, kc, vc, near, near_sm, part, came,
                  own_l, sib_s, sib_r, zs, zr, ys, yr, near_s, near_r, near_l, z_load, y_load,
                  part_s, part_r, full_s, full_r):
    y, z, core = place()
    mp = lax.axis_index("mp")
    sib = index_of(y, z, 1 - core)
    z_peer = (index_of(y, z + 1, core), index_of(y, z - 1, core))
    y_peer = (index_of(y + 1, z, core), index_of(y - 1, z, core))
    line = [index_of(y, z + s, core) for s in range(1, NZ)]
    line += [index_of(y, z + s, 1 - core) for s in range(NZ)]
    barrier = pltpu.get_barrier_semaphore()
    for s in range(1, NX):
        pl.semaphore_signal(
            barrier, inc=1, device_id={"mp": lax.rem(mp + s, NX)}, device_id_type=MESH)
    for peer in line + list(y_peer):
        pl.semaphore_signal(barrier, inc=1, device_id={"seq": peer}, device_id_type=MESH)
    pl.semaphore_wait(barrier, NX - 1 + len(line) + len(y_peer))
    mine = z * NC + core
    near_x = [
        pltpu.make_async_remote_copy(
            src_ref=lists, dst_ref=near.at[mine, mp], send_sem=near_s.at[s - 1],
            recv_sem=near_r.at[s - 1], device_id={"mp": lax.rem(mp + s, NX)}, device_id_type=MESH)
        for s in range(1, NX)
    ]
    near_line = [
        remote(near.at[mine], near.at[mine], near_s.at[NX - 1 + n], near_r.at[NX - 1 + n], peer)
        for n, peer in enumerate(line)
    ]
    own = pl.ds(pl.multiple_of(core * HALF, HALF), HALF)
    other = pl.ds(pl.multiple_of((1 - core) * HALF, HALF), HALF)
    sources = (q, g, k, v)
    gathered = (qa, ga, ka, va)
    here = (qc, gc, kc, vc)
    side = (core, 1 - core)

    def z_at(d, t):
        return lax.rem(z + (2 * d - 1) * t + NZ, NZ)

    def y_at(d, t):
        return lax.rem(y + (2 * d - 1) * t + NY, NY)

    def z_copy(d, a, t):
        dst = gathered[a].at[z_at(d, t), side[d]]
        src = sources[a].at[:, :, own] if (t == 0 and d == 0) else dst
        return remote(src, dst, zs.at[d, a, t], zr.at[d, a, t], z_peer[d])

    def y_copy(d, a, t):
        dst = gathered[2 + a].at[y_at(d, t), side[d]]
        src = sources[2 + a].at[:, :, own] if (t == 0 and d == 0) else dst
        return remote(src, dst, ys.at[d, a, t], yr.at[d, a, t], y_peer[d])

    def z_in(d, a, t):
        src = sources[a].at[:, :, own] if (t == 0 and d == 0) else gathered[a].at[z_at(d, t), side[d]]
        return pltpu.make_async_copy(src, here[a].at[z_at(d, t) * NC + side[d]], z_load.at[d, a, t])

    def y_in(d, a, t):
        src = sources[2 + a].at[:, :, own] if (t == 0 and d == 0) else gathered[2 + a].at[y_at(d, t), side[d]]
        return pltpu.make_async_copy(src, here[2 + a].at[y_at(d, t) * NC + side[d]], y_load.at[d, a, t])

    at = (z, z, y, y)
    sibling = [
        remote(sources[a].at[:, :, other], gathered[a].at[at[a], core], sib_s.at[a], sib_r.at[a], sib)
        for a in range(4)
    ]
    for a in range(2):
        z_copy(0, a, 0).start()
    for copy in sibling[:2]:
        copy.start()
    for a in range(2):
        y_copy(0, a, 0).start()
    for copy in sibling[2:]:
        copy.start()
    for copy in near_x:
        copy.start()
    local = [
        pltpu.make_async_copy(sources[a].at[:, :, own], gathered[a].at[at[a], core], own_l.at[a])
        for a in range(4)
    ]
    for copy in local:
        copy.start()
    for a in range(2):
        z_in(0, a, 0).start()
        y_in(0, a, 0).start()
    near[mine, mp] = lists[...]
    for a in range(2):
        sibling[a].wait_recv()
        z_copy(1, a, 0).start()
        z_in(1, a, 0).start()
    for a in range(2):
        sibling[2 + a].wait_recv()
        y_copy(1, a, 0).start()
        y_in(1, a, 0).start()
    for copy in near_x:
        copy.wait_recv()
    for copy in near_line:
        copy.start()
    for copy in near_line:
        copy.wait_recv()
    listed = pltpu.make_async_copy(near, near_sm, near_l)
    listed.start()
    listed.wait()

    def look_up(slot, carry):
        source, owner = slot // OWNERS_HERE, lax.rem(slot, OWNERS_HERE)
        wanted = ((owner // NC) * NZ + z) * NC + lax.rem(owner, NC)
        found = jnp.int32(0)
        hit = jnp.int32(0)
        for item in range(CH * NBR):
            r = near_sm[source, item // (CH * NBR // NX), 0, item % (CH * NBR // NX)]
            same = (r // ROWS == wanted).astype(jnp.int32)
            found = found + same * (item // NBR * ROWS + lax.rem(r, ROWS) - found)
            hit = hit + same
        table[slot] = found
        hits[slot] = hit
        return carry

    lax.fori_loop(0, SOURCES * OWNERS_HERE, look_up, 0)

    def part_stats(first_source, last_source, first_owner, last_owner):
        owners = last_owner - first_owner

        def one(n, carry):
            a = first_source + n // owners
            b = first_owner + lax.rem(n, owners)
            source_z = z_at(lax.rem(a, 2), a // 2)
            source_core = lax.rem(core + a, NC)
            source = source_z * NC + source_core
            owner = y_at(lax.rem(b, 2), b // 2) * NC + lax.rem(core + b, NC)
            found = table[source * OWNERS_HERE + owner]
            span, row = found // ROWS, lax.rem(found, ROWS)
            tops, crosses = [], []
            for pair in range(PAIRS):
                columns = slice(pair * PAIR, (pair + 1) * PAIR)
                scores = dot(kc[owner, row, :, columns], diagonal(qc[source, span, :, columns]), NT) * SCALE
                grad_p = dot(vc[owner, row, :, columns], diagonal(gc[source, span, :, columns]), NT)
                highest = jnp.max(scores, axis=0, keepdims=True)
                expons = jnp.exp(scores - highest)
                total = jnp.sum(expons, axis=0, keepdims=True)
                cross = jnp.sum(expons * grad_p, axis=0, keepdims=True)
                tops.append(highest + jnp.log(total))
                crosses.append(cross / total)
            part[source_z, source_core, owner, 0] = jnp.concatenate(tops, axis=0)
            part[source_z, source_core, owner, 1] = jnp.concatenate(crosses, axis=0)
            return carry

        lax.fori_loop(0, (last_source - first_source) * owners, one, 0)

    def part_copy(n):
        d, t = n % 2, n // 2
        block = part.at[z_at(d, t), side[d]]
        return remote(block, came.at[z, side[d]], part_s.at[n - 2], part_r.at[n - 2], index_of(y, z_at(d, t), core))

    def arrived(copy, d, a, t, steps):
        copy(d, a, t - 1).wait_recv()
        if t < steps - 1:
            copy(d, a, t).start()

    def each(into, t, act):
        for d in range(2):
            for a in range(2):
                act(into(d, a, t))

    def load(copy):
        copy.start()

    def loaded(copy):
        copy.wait()

    each(z_in, 0, loaded)
    each(y_in, 0, loaded)
    last = 2 * (NZ - 1)
    for t in range(1, NZ):
        ready = 2 * ((t - 1) // 2 + 1)
        ends = t == NZ - 1
        if not ends:
            for d in range(2):
                arrived(z_copy, d, 0, t, NZ)
        if t > 1:
            each(z_in, t - 1, loaded)
        if t > 1 and t % 2 == 1:
            each(y_in, t // 2, loaded)
            part_stats(0, 2 * (t - 1), ready - 2, ready)
        part_stats(2 * (t - 1), 2 * t, 0, ready)
        if ends:
            for n in range(2, last):
                part_copy(n).start()
            for d in range(2):
                arrived(z_copy, d, 0, t, NZ)
        for d in range(2):
            arrived(z_copy, d, 1, t, NZ)
        each(z_in, t, load)
        if t % 2 == 0:
            for a in range(2):
                for d in range(2):
                    arrived(y_copy, d, a, t // 2, NY)
            each(y_in, t // 2, load)
    each(z_in, NZ - 1, loaded)
    part_stats(last, last + 2, 0, 2 * NY)
    for n in range(last, last + 2):
        part_copy(n).start()
    came[z] = part[z]
    for n in range(2, last + 2):
        part_copy(n).wait_recv()

    def merge(n, carry):
        source_core, span = n // CH, lax.rem(n, CH)
        sides = []
        for item in range(NBR):
            r = near_sm[z * NC + source_core, span // 2, 0, lax.rem(span, 2) * NBR + item]
            holder = r // ROWS
            sides.append(came[lax.rem(holder // NC, NZ), source_core,
                              holder // (NC * NZ) * NC + lax.rem(holder, NC)])
        peak = jnp.maximum(sides[0][0], sides[1][0])
        weights = [jnp.exp(one[0] - peak) for one in sides]
        total = weights[0] + weights[1]
        full[z, 0, n] = peak + jnp.log(total)
        full[z, 1, n] = (weights[0] * sides[0][1] + weights[1] * sides[1][1]) / total
        return carry

    lax.fori_loop(0, NC * CH, merge, 0)
    back = [
        remote(full.at[z], full.at[z], full_s.at[s - 1], full_r.at[s - 1], index_of(y, z + s, core))
        for s in range(1, NZ)
    ]
    for copy in back:
        copy.start()
    for copy in back:
        copy.wait_recv()
    for copy in local:
        copy.wait()
    for copy in near_x + near_line + sibling + back:
        copy.wait_send()
    for n in range(2, last + 2):
        part_copy(n).wait_send()
    for d in range(2):
        for a in range(2):
            for t in range(NZ - 1):
                z_copy(d, a, t).wait_send()
            for t in range(NY - 1):
                y_copy(d, a, t).wait_send()


def gather(q, g, k, v, lists):
    sem = pltpu.SemaphoreType.DMA
    vmem = pl.BlockSpec(memory_space=pltpu.VMEM)
    part_shape = (NZ, NC, OWNERS_HERE, 2, PAIRS, HEAD)
    near_shape = (SOURCES, NX, 1, 128)
    near_count = NX - 1 + SOURCES - 1
    return pl.pallas_call(
        gather_kernel,
        out_shape=(
            jax.ShapeDtypeStruct((NZ, NC, CH, SPAN, HALF), bf16),
            jax.ShapeDtypeStruct((NZ, NC, CH, SPAN, HALF), bf16),
            jax.ShapeDtypeStruct((NY, NC, ROWS, NLEN, HALF), bf16),
            jax.ShapeDtypeStruct((NY, NC, ROWS, NLEN, HALF), bf16),
            jax.ShapeDtypeStruct((SOURCES * OWNERS_HERE,), jnp.int32),
            jax.ShapeDtypeStruct((SOURCES * OWNERS_HERE,), jnp.int32),
            jax.ShapeDtypeStruct(STAT_SHAPE, f32),
        ),
        in_specs=[ANY] * 4 + [vmem],
        out_specs=(ANY,) * 4 + (SMEM, SMEM, vmem),
        scratch_shapes=[
            pltpu.VMEM((SOURCES, CH, SPAN, HALF), bf16),
            pltpu.VMEM((SOURCES, CH, SPAN, HALF), bf16),
            pltpu.VMEM((OWNERS_HERE, ROWS, NLEN, HALF), bf16),
            pltpu.VMEM((OWNERS_HERE, ROWS, NLEN, HALF), bf16),
            pltpu.VMEM(near_shape, jnp.int32),
            pltpu.SMEM(near_shape, jnp.int32),
            pltpu.VMEM(part_shape, f32),
            pltpu.VMEM(part_shape, f32),
            sem((4,)),
            sem((4,)),
            sem((4,)),
            sem((2, 2, NZ - 1)),
            sem((2, 2, NZ - 1)),
            sem((2, 2, NY - 1)),
            sem((2, 2, NY - 1)),
            sem((near_count,)),
            sem((near_count,)),
            sem,
            sem((2, 2, NZ)),
            sem((2, 2, NY)),
            sem((2 * NZ - 2,)),
            sem((2 * NZ - 2,)),
            sem((NZ - 1,)),
            sem((NZ - 1,)),
        ],
        compiler_params=pltpu.CompilerParams(
            collective_id=0, has_side_effects=True, vmem_limit_bytes=56 * 2**20),
        name="gather_blocks",
    )(q, g, k, v, lists)


def whole(shape, **more):
    return pl.BlockSpec(shape, lambda *_: (0,) * len(shape), **more)


SMEM = pl.BlockSpec(memory_space=pltpu.SMEM)
ROW_BLOCK = pl.BlockSpec((ROWS, NLEN, HALF), lambda n: (n, 0, 0))
SPAN_BLOCK = whole((SPANS_HERE, SPAN, HALF), pipeline_mode=pl.Buffered(1))
STAT_SHAPE = (NZ, 2, NC * CH, PAIRS, HEAD)


def grads_kernel(table, hits, q, g, k, v, stat, dq, dk, dv, dk_acc, dv_acc):
    owner = pl.program_id(0)

    @pl.when(owner == 0)
    def _():
        def clear(n, carry):
            dq[n] = jnp.zeros((SPAN, HALF), bf16)
            return carry

        lax.fori_loop(0, SPANS_HERE, clear, 0)

    def fresh(n, carry):
        dk_acc[n] = jnp.zeros((NLEN, HALF), f32)
        dv_acc[n] = jnp.zeros((NLEN, HALF), f32)
        return carry

    lax.fori_loop(0, ROWS, fresh, 0)

    def item(source, carry):
        slot = source * OWNERS_HERE + owner

        @pl.when(hits[slot] > 0)
        def _():
            found = table[slot]
            local, row = lax.rem(source, NC) * CH + found // ROWS, lax.rem(found, ROWS)
            span = source * CH + found // ROWS
            log_total = stat[source // NC, 0, local]
            delta = stat[source // NC, 1, local]
            for pair in range(PAIRS):
                columns = slice(pair * PAIR, (pair + 1) * PAIR)
                keys, values = k[row, :, columns], v[row, :, columns]
                queries, grads = diagonal(q[span, :, columns]), diagonal(g[span, :, columns])
                scores = dot(keys, queries, NT) * SCALE
                probs = jnp.exp(scores - log_total[pair:pair + 1])
                grad_p = dot(values, grads, NT)
                grad_s = (probs * (grad_p - delta[pair:pair + 1]) * SCALE).astype(bf16)
                dv_acc[row, :, columns] += dot(probs.astype(bf16), grads, NN)
                dk_acc[row, :, columns] += dot(grad_s, queries, NN)
                more = dot(grad_s, keys, TN)
                more = jnp.concatenate([more[:SPAN, :HEAD], more[SPAN:, HEAD:]], axis=1)
                more = more.astype(bf16).astype(f32)
                dq[span, :, columns] = (dq[span, :, columns].astype(f32) + more).astype(bf16)

        return carry

    lax.fori_loop(0, SOURCES, item, 0)

    def settle(n, carry):
        dk[n] = dk_acc[n].astype(bf16)
        dv[n] = dv_acc[n].astype(bf16)
        return carry

    lax.fori_loop(0, ROWS, settle, 0)


def grads(table, hits, qa, ga, ka, va, stat):
    return pl.pallas_call(
        grads_kernel,
        grid=(OWNERS_HERE,),
        out_shape=(
            jax.ShapeDtypeStruct((SPANS_HERE, SPAN, HALF), bf16),
            jax.ShapeDtypeStruct((ROWS_HERE, NLEN, HALF), bf16),
            jax.ShapeDtypeStruct((ROWS_HERE, NLEN, HALF), bf16),
        ),
        in_specs=[SMEM, SMEM, SPAN_BLOCK, SPAN_BLOCK, ROW_BLOCK, ROW_BLOCK, whole(STAT_SHAPE)],
        out_specs=(whole((SPANS_HERE, SPAN, HALF)), ROW_BLOCK, ROW_BLOCK),
        scratch_shapes=[pltpu.VMEM((ROWS, NLEN, HALF), f32)] * 2,
        compiler_params=pltpu.CompilerParams(vmem_limit_bytes=56 * 2**20),
        name="part_grads",
    )(table, hits, qa, ga, ka, va, stat)


def reduce_kernel(dqp, dkp, dvp, dq, dk, dv, z_in, z_own, y_in, y_own,
                  zl, yl, zs, zr, ys, yr, out_s, out_r, out_l):
    y, z, core = place()
    sib = index_of(y, z, 1 - core)
    z_peer = (index_of(y, z + 1, core), index_of(y, z - 1, core))
    y_peer = (index_of(y + 1, z, core), index_of(y - 1, z, core))
    greet((sib,) + z_peer + y_peer)
    own = pl.ds(pl.multiple_of(core * HALF, HALF), HALF)
    y_src = (dkp, dvp)
    side = (1 - core, core)

    def z_block(d, t):
        return lax.rem(z - 1 - t + 2 * NZ, NZ) if d == 0 else lax.rem(z + 1 + t, NZ)

    def y_block(d, t):
        return lax.rem(y - 1 - t + 2 * NY, NY) if d == 0 else lax.rem(y + 1 + t, NY)

    def z_copy(d, t):
        src = dqp.at[z_block(d, 0), side[d]] if t == 0 else z_in.at[d, t - 1]
        return remote(src, z_in.at[d, t], zs.at[d, t], zr.at[d, t], z_peer[d])

    def y_copy(d, sub, t):
        src = y_src[d].at[y_block(d, 0), side[sub]] if t == 0 else y_in.at[d, sub, t - 1]
        return remote(src, y_in.at[d, sub, t], ys.at[d, sub, t], yr.at[d, sub, t], y_peer[d])

    def z_load(d, t):
        return pltpu.make_async_copy(dqp.at[z_block(d, t + 1), side[d]], z_own.at[d, t], zl.at[d, t])

    def y_load(d, sub, t):
        return pltpu.make_async_copy(
            y_src[d].at[y_block(d, t + 1), side[sub]], y_own.at[d, sub, t], yl.at[d, sub, t])

    for d in range(2):
        y_copy(d, 0, 0).start()
    for d in range(2):
        z_copy(d, 0).start()
    for d in range(2):
        y_copy(d, 1, 0).start()
    for t in range(NY - 1):
        for sub in range(2):
            for d in range(2):
                y_load(d, sub, t).start()
    for t in range(NZ - 1):
        for d in range(2):
            z_load(d, t).start()

    def add(total, more, count):
        def one(n, carry):
            total[n] = (total[n].astype(f32) + more[n].astype(f32)).astype(bf16)
            return carry

        lax.fori_loop(0, count, one, 0)

    def finish(which, out, src):
        there = remote(src[0], out.at[:, :, own], out_s.at[which], out_r.at[which], sib)
        here = pltpu.make_async_copy(src[1], out.at[:, :, own], out_l.at[which])
        return there, here

    ends = (
        finish(0, dk, (y_in.at[0, 0, NY - 2], y_in.at[0, 1, NY - 2])),
        finish(1, dv, (y_in.at[1, 0, NY - 2], y_in.at[1, 1, NY - 2])),
        finish(2, dq, (z_in.at[0, NZ - 2], z_in.at[1, NZ - 2])),
    )

    def z_step(t):
        for d in range(2):
            z_copy(d, t).wait_recv()
            z_load(d, t).wait()
            add(z_in.at[d, t], z_own.at[d, t], CH)
            if t < NZ - 2:
                z_copy(d, t + 1).start()
            else:
                ends[2][d].start()

    def y_step(t, sub):
        for d in range(2):
            y_copy(d, sub, t).wait_recv()
            y_load(d, sub, t).wait()
            add(y_in.at[d, sub, t], y_own.at[d, sub, t], ROWS)
            if t < NY - 2:
                y_copy(d, sub, t + 1).start()
            else:
                ends[d][sub].start()

    z_step(0)
    y_step(0, 0)
    z_step(1)
    y_step(0, 1)
    z_step(2)
    y_step(1, 0)
    z_step(3)
    z_step(4)
    y_step(1, 1)
    z_step(5)
    y_step(2, 0)
    z_step(6)
    y_step(2, 1)
    for there, here in ends:
        there.wait()
        here.wait()
    for d in range(2):
        for t in range(NZ - 1):
            z_copy(d, t).wait_send()
        for sub in range(2):
            for t in range(NY - 1):
                y_copy(d, sub, t).wait_send()


def reduce(dqp, dkp, dvp):
    sem = pltpu.SemaphoreType.DMA
    return pl.pallas_call(
        reduce_kernel,
        out_shape=(
            jax.ShapeDtypeStruct((CH, SPAN, WIDE), bf16),
            jax.ShapeDtypeStruct((ROWS, NLEN, WIDE), bf16),
            jax.ShapeDtypeStruct((ROWS, NLEN, WIDE), bf16),
        ),
        in_specs=[ANY] * 3,
        out_specs=(ANY,) * 3,
        scratch_shapes=[
            pltpu.VMEM((2, NZ - 1, CH, SPAN, HALF), bf16),
            pltpu.VMEM((2, NZ - 1, CH, SPAN, HALF), bf16),
            pltpu.VMEM((2, 2, NY - 1, ROWS, NLEN, HALF), bf16),
            pltpu.VMEM((2, 2, NY - 1, ROWS, NLEN, HALF), bf16),
            sem((2, NZ - 1)),
            sem((2, 2, NY - 1)),
            sem((2, NZ - 1)),
            sem((2, NZ - 1)),
            sem((2, 2, NY - 1)),
            sem((2, 2, NY - 1)),
            sem((3,)),
            sem((3,)),
            sem((3,)),
        ],
        compiler_params=pltpu.CompilerParams(
            collective_id=2, has_side_effects=True, vmem_limit_bytes=56 * 2**20),
        name="reduce_blocks",
    )(dqp, dkp, dvp)


def per_device(queries, out_grad, row_keys, row_values, neighbours):
    few = neighbours.size
    lists = jnp.pad(neighbours.reshape(1, few), ((0, 0), (0, 128 - few)))
    qa, ga, ka, va, table, hits, full = gather(queries, out_grad, row_keys, row_values, lists)
    dqp, dkp, dvp = grads(
        table,
        hits,
        qa.reshape(SPANS_HERE, SPAN, HALF),
        ga.reshape(SPANS_HERE, SPAN, HALF),
        ka.reshape(ROWS_HERE, NLEN, HALF),
        va.reshape(ROWS_HERE, NLEN, HALF),
        full,
    )
    return reduce(
        dqp.reshape(NZ, NC, CH, SPAN, HALF),
        dkp.reshape(NY, NC, ROWS, NLEN, HALF),
        dvp.reshape(NY, NC, ROWS, NLEN, HALF),
    )


def solution(mesh):
    in_specs = (
        P("seq", None, "mp"),
        P("seq", None, "mp"),
        P("seq", None, "mp"),
        P("seq", None, "mp"),
        P(("seq", "mp"), None),
    )
    out_specs = (P("seq", None, "mp"), P("seq", None, "mp"), P("seq", None, "mp"))
    return jax.shard_map(
        per_device, mesh=mesh, in_specs=in_specs, out_specs=out_specs, check_vma=False
    )
```

time: 427 us -> 414 us (0.970)
  Pallas kernels: 412 us -> 398 us
    pallas_call x2 -> x0, Pallas kernels: 51.3 us -> none  [the longest x1 27.4 us: combine(): pl.pallas_call(combine_kernel, out_shape=jax.ShapeDtypeStruct(STAT_SHAPE,...]
    pallas_call x1, Pallas kernels: 171 us -> 209 us  [gather(): pl.pallas_call(gather_kernel, out_shape=(jax.ShapeDtypeStruct((NZ, NC, CH...]
    pallas_call x1, Pallas kernels: 157 us -> 149 us  [reduce(): pl.pallas_call(reduce_kernel, out_shape=(jax.ShapeDtypeStruct((CH, SPAN,...]
    pallas_call x1, Pallas kernels: 33 us -> 39 us  [grads(): pl.pallas_call(grads_kernel, grid=(OWNERS_HERE,), out_shape=(jax.ShapeDty...]
    unnamed x9 -> x3, local copies, waits for them, and re-layouts: 10.1 us -> 8.42 us
where the time goes in v3:
time: 414 us; the launch traced here: 408 us
  Pallas kernels  398 us (96%)
  local copies, waits for them, and re-layouts  9.7 us (2%)
    pallas_call x1, Pallas kernels, gather(): pl.pallas_call(gather_kernel, out_shape=(jax.ShapeDtypeStruct((NZ, NC, CH...  209 us
    pallas_call x1, Pallas kernels, reduce(): pl.pallas_call(reduce_kernel, out_shape=(jax.ShapeDtypeStruct((CH, SPAN,...  149 us
    pallas_call x1, Pallas kernels, grads(): pl.pallas_call(grads_kernel, grid=(OWNERS_HERE,), out_shape=(jax.ShapeDty...  39 us
    unnamed x3, local copies, waits for them, and re-layouts  8.42 us

profile of v3, /device:TPU:1, one launch (start us, length us, event | category | flops | bytes accessed | tf_op | source)
XLA Modules:
  0.0 408.1 jit_solution(8570533524506126659)
XLA Ops:
  0.6 0.8 reshape.30
  1.4 0.5 pad.4.lists
  1.9 209.4 %gather_blocks.1 = (bf16[8,2,8,64,512]{4,3,2,1,0:T(8,128)(2,1)}, bf16[8,2,8,64,512]{4,3,2,1,0:T(8,128)(2,1)}, bf16[4,2,8,128,512]{4,3,2,1,0:T(8,128)(2,1)}, bf16...) custom-call(bf16[8,64,1024]{2,1,0:T(8,128)(2,1)} %q.1, ...), custom_call_target="tpu_custom_call" | custom-call | tf_op jit(solution)/shard_map/gather_blocks/pallas_call | solution.py:319
  211.4 39.0 %part_grads.1 = (bf16[128,64,512]{2,1,0:T(8,128)(2,1)}, bf16[64,128,512]{2,1,0:T(8,128)(2,1)}, bf16[64,128,512]{2,1,0:T(8,128)(2,1)}) custom-call(s32[128]{0:T(128)} %get-tuple-element.13.table, s32[128]{0:T(128)} %get-tuple-element.14.hits, bf16[128,64,512]{2,1,0:T(8,128)(2,1)} %bitcast.10, bf16[128,64,512]{2,1,0:T(8,128)(2,1)} %bitcast.11, ...), custom_call_target="tpu_custom_call" | custom-call | tf_op jit(solution)/shard_map/part_grads/pallas_call | solution.py:430
  250.4 149.3 %reduce_blocks.1 = (bf16[8,64,1024]{2,1,0:T(8,128)(2,1)}, bf16[8,128,1024]{2,1,0:T(8,128)(2,1)}, bf16[8,128,1024]{2,1,0:T(8,128)(2,1)}) custom-call(bf16[8,2,8,64,512]{4,3,2,1,0:T(8,128)(2,1)} %bitcast.7, bf16[4,2,8,128,512]{4,3,2,1,0:T(8,128)(2,1)} %bitcast.8, bf16[4,2,8,128,512]{4,3,2,1,0:T(8,128)(2,1)} %bitcast.9), custom_call_target="tpu_custom_call" | custom-call | tf_op jit(solution)/shard_map/reduce_blocks/pallas_call | solution.py:556
  399.7 2.3 copy.11
  402.0 3.1 copy.12
  405.1 3.1 copy.13

commit v4 on v3

v4 whole, which is shorter than its diff:
```python
import jax
import jax.numpy as jnp
from jax import lax
from jax.experimental import pallas as pl
from jax.experimental.pallas import tpu as pltpu
from jax.sharding import PartitionSpec as P

HEAD = 128
UNROLL = 4
SPAN = 64
NLEN = 128
NBR = 2
NX, NY, NZ, NC = 4, 4, 8, 2
CH, ROWS = 8, 8
WIDE = 1024
HALF = WIDE // NC
PAIR = 2 * HEAD
PAIRS = HALF // PAIR
SOURCES = NZ * NC
SPANS_HERE = SOURCES * CH
OWNERS_HERE = NY * NC
ROWS_HERE = OWNERS_HERE * ROWS
SLOTS = SOURCES * OWNERS_HERE
SCALE = HEAD ** (-0.5)
MESH = pl.DeviceIdType.MESH
ANY = pl.BlockSpec(memory_space=pl.ANY)
f32, bf16 = jnp.float32, jnp.bfloat16


def place():
    me = lax.axis_index("seq")
    core = lax.rem(me, NC)
    z = lax.rem(me // NC, NZ)
    y = me // (NC * NZ)
    return y, z, core


def index_of(y, z, core):
    return (lax.rem(y + NY, NY) * NZ + lax.rem(z + NZ, NZ)) * NC + core


def greet(peers):
    barrier = pltpu.get_barrier_semaphore()
    for peer in peers:
        pl.semaphore_signal(barrier, inc=1, device_id={"seq": peer}, device_id_type=MESH)
    pl.semaphore_wait(barrier, len(peers))


def remote(src, dst, send_sem, recv_sem, peer):
    return pltpu.make_async_remote_copy(
        src_ref=src, dst_ref=dst, send_sem=send_sem, recv_sem=recv_sem,
        device_id={"seq": peer}, device_id_type=MESH)


NT = ((1,), (1,))
NN = ((1,), (0,))
TN = ((0,), (0,))


def dot(a, b, dims):
    return lax.dot_general(a, b, (dims, ((), ())), preferred_element_type=f32)


def diagonal(both):
    blank = jnp.zeros((SPAN, HEAD), both.dtype)
    return jnp.concatenate([
        jnp.concatenate([both[:, :HEAD], blank], axis=1),
        jnp.concatenate([blank, both[:, HEAD:]], axis=1),
    ], axis=0)


def gather_kernel(q, g, k, v, lists, qa, ga, ka, va, table, hits, order, same, ends, slots, full,
                  qc, gc, kc, vc, near, near_sm, keys, ranks, part, came,
                  own_l, sib_s, sib_r, zs, zr, ys, yr, near_s, near_r, near_l, z_load, y_load,
                  part_s, part_r, full_s, full_r):
    y, z, core = place()
    mp = lax.axis_index("mp")
    sib = index_of(y, z, 1 - core)
    z_peer = (index_of(y, z + 1, core), index_of(y, z - 1, core))
    y_peer = (index_of(y + 1, z, core), index_of(y - 1, z, core))
    line = [index_of(y, z + s, core) for s in range(1, NZ)]
    line += [index_of(y, z + s, 1 - core) for s in range(NZ)]
    barrier = pltpu.get_barrier_semaphore()
    for s in range(1, NX):
        pl.semaphore_signal(
            barrier, inc=1, device_id={"mp": lax.rem(mp + s, NX)}, device_id_type=MESH)
    for peer in line + list(y_peer):
        pl.semaphore_signal(barrier, inc=1, device_id={"seq": peer}, device_id_type=MESH)
    pl.semaphore_wait(barrier, NX - 1 + len(line) + len(y_peer))
    mine = z * NC + core
    near_x = [
        pltpu.make_async_remote_copy(
            src_ref=lists, dst_ref=near.at[mine, mp], send_sem=near_s.at[s - 1],
            recv_sem=near_r.at[s - 1], device_id={"mp": lax.rem(mp + s, NX)}, device_id_type=MESH)
        for s in range(1, NX)
    ]
    near_line = [
        remote(near.at[mine], near.at[mine], near_s.at[NX - 1 + n], near_r.at[NX - 1 + n], peer)
        for n, peer in enumerate(line)
    ]
    own = pl.ds(pl.multiple_of(core * HALF, HALF), HALF)
    other = pl.ds(pl.multiple_of((1 - core) * HALF, HALF), HALF)
    sources = (q, g, k, v)
    gathered = (qa, ga, ka, va)
    here = (qc, gc, kc, vc)
    side = (core, 1 - core)

    def z_at(d, t):
        return lax.rem(z + (2 * d - 1) * t + NZ, NZ)

    def y_at(d, t):
        return lax.rem(y + (2 * d - 1) * t + NY, NY)

    def z_copy(d, a, t):
        dst = gathered[a].at[z_at(d, t), side[d]]
        src = sources[a].at[:, :, own] if (t == 0 and d == 0) else dst
        return remote(src, dst, zs.at[d, a, t], zr.at[d, a, t], z_peer[d])

    def y_copy(d, a, t):
        dst = gathered[2 + a].at[y_at(d, t), side[d]]
        src = sources[2 + a].at[:, :, own] if (t == 0 and d == 0) else dst
        return remote(src, dst, ys.at[d, a, t], yr.at[d, a, t], y_peer[d])

    def z_in(d, a, t):
        src = sources[a].at[:, :, own] if (t == 0 and d == 0) else gathered[a].at[z_at(d, t), side[d]]
        return pltpu.make_async_copy(src, here[a].at[z_at(d, t) * NC + side[d]], z_load.at[d, a, t])

    def y_in(d, a, t):
        src = sources[2 + a].at[:, :, own] if (t == 0 and d == 0) else gathered[2 + a].at[y_at(d, t), side[d]]
        return pltpu.make_async_copy(src, here[2 + a].at[y_at(d, t) * NC + side[d]], y_load.at[d, a, t])

    at = (z, z, y, y)
    sibling = [
        remote(sources[a].at[:, :, other], gathered[a].at[at[a], core], sib_s.at[a], sib_r.at[a], sib)
        for a in range(4)
    ]
    for copy in near_x:
        copy.start()
    for a in range(2):
        z_copy(0, a, 0).start()
    for copy in sibling[:2]:
        copy.start()
    for a in range(2):
        y_copy(0, a, 0).start()
    for copy in sibling[2:]:
        copy.start()
    local = [
        pltpu.make_async_copy(sources[a].at[:, :, own], gathered[a].at[at[a], core], own_l.at[a])
        for a in range(4)
    ]
    for copy in local:
        copy.start()
    for a in range(2):
        z_in(0, a, 0).start()
        y_in(0, a, 0).start()
    near[mine, mp] = lists[...]
    for a in range(2):
        sibling[a].wait_recv()
        z_copy(1, a, 0).start()
        z_in(1, a, 0).start()
    for a in range(2):
        sibling[2 + a].wait_recv()
        y_copy(1, a, 0).start()
        y_in(1, a, 0).start()
    listed = pltpu.make_async_copy(near, near_sm, near_l)

    def look_up(slot, carry):
        source, owner = slot // OWNERS_HERE, lax.rem(slot, OWNERS_HERE)
        wanted = ((owner // NC) * NZ + z) * NC + lax.rem(owner, NC)
        found = jnp.int32(0)
        hit = jnp.int32(0)
        for item in range(CH * NBR):
            r = near_sm[source, item // (CH * NBR // NX), 0, item % (CH * NBR // NX)]
            same = (r // ROWS == wanted).astype(jnp.int32)
            found = found + same * (item // NBR * ROWS + lax.rem(r, ROWS) - found)
            hit = hit + same
        table[slot] = found
        hit = (hit > 0).astype(jnp.int32)
        hits[slot] = hit
        none = ROWS * SOURCES
        keys[owner * SOURCES + source] = source + none + hit * (lax.rem(found, ROWS) * SOURCES - none)
        return carry

    def rank(n, carry):
        first = n // SOURCES * SOURCES
        mine = keys[n]
        below = jnp.int32(0)
        for other_one in range(SOURCES):
            below = below + (keys[first + other_one] < mine).astype(jnp.int32)
        ranks[n] = below
        return carry

    def put_in_order(n, carry):
        first, at_n = n // SOURCES * SOURCES, lax.rem(n, SOURCES)
        chosen = jnp.int32(0)
        for one in range(SOURCES):
            chosen = chosen + one * (ranks[first + one] == at_n).astype(jnp.int32)
        order[n] = chosen
        return carry

    def mark_same(n, carry):
        first, at_n = n // SOURCES * SOURCES, lax.rem(n, SOURCES)
        now = keys[first + order[n]] // SOURCES
        before = keys[first + order[first + lax.rem(at_n + SOURCES - 1, SOURCES)]] // SOURCES
        same[n] = (now == before).astype(jnp.int32) * ((at_n + SOURCES - 1) // SOURCES)
        return carry

    def mark_end(n, carry):
        first, row = n // ROWS * SOURCES, lax.rem(n, ROWS)
        below = jnp.int32(0)
        upto = jnp.int32(0)
        for one in range(SOURCES):
            key = keys[first + one]
            below = below + (key < row * SOURCES).astype(jnp.int32)
            upto = upto + (key < (row + 1) * SOURCES).astype(jnp.int32)
        ends[n] = upto * (upto > below).astype(jnp.int32)
        return carry

    def mark_slot(n, carry):
        source, item = n // (CH * NBR), lax.rem(n, CH * NBR)
        each_x = CH * NBR // NX
        holder = near_sm[source, item // each_x, 0, lax.rem(item, each_x)] // ROWS
        local = (lax.rem(holder // NC, NZ) == z).astype(jnp.int32)
        first = (holder // (NC * NZ) * NC + lax.rem(holder, NC)) * SOURCES
        slots[n] = SLOTS + local * (first + ranks[first + source] - SLOTS)
        return carry

    def part_stats(first_source, last_source, first_owner, last_owner):
        owners = last_owner - first_owner

        def one(n):
            a = first_source + n // owners
            b = first_owner + lax.rem(n, owners)
            source_z = z_at(lax.rem(a, 2), a // 2)
            source_core = lax.rem(core + a, NC)
            source = source_z * NC + source_core
            owner = y_at(lax.rem(b, 2), b // 2) * NC + lax.rem(core + b, NC)
            found = table[source * OWNERS_HERE + owner]
            span, row = found // ROWS, lax.rem(found, ROWS)
            tops, crosses = [], []
            for pair in range(PAIRS):
                columns = slice(pair * PAIR, (pair + 1) * PAIR)
                scores = dot(kc[owner, row, :, columns], diagonal(qc[source, span, :, columns]), NT) * SCALE
                grad_p = dot(vc[owner, row, :, columns], diagonal(gc[source, span, :, columns]), NT)
                highest = jnp.max(scores, axis=0, keepdims=True)
                expons = jnp.exp(scores - highest)
                total = jnp.sum(expons, axis=0, keepdims=True)
                cross = jnp.sum(expons * grad_p, axis=0, keepdims=True)
                tops.append(highest + jnp.log(total))
                crosses.append(cross / total)
            return source_z, source_core, owner, tops, crosses

        def some(n, carry):
            results = [one(2 * n + more) for more in range(2)]
            for source_z, source_core, owner, tops, crosses in results:
                part[source_z, source_core, owner, 0] = jnp.concatenate(tops, axis=0)
                part[source_z, source_core, owner, 1] = jnp.concatenate(crosses, axis=0)
            return carry

        lax.fori_loop(0, (last_source - first_source) * owners // 2, some, 0)

    def part_copy(n):
        d, t = n % 2, n // 2
        block = part.at[z_at(d, t), side[d]]
        return remote(block, came.at[z, side[d]], part_s.at[n - 2], part_r.at[n - 2], index_of(y, z_at(d, t), core))

    def arrived(copy, d, a, t, steps):
        copy(d, a, t - 1).wait_recv()
        if t < steps - 1:
            copy(d, a, t).start()

    def each(into, t, act):
        for d in range(2):
            for a in range(2):
                act(into(d, a, t))

    def load(copy):
        copy.start()

    def loaded(copy):
        copy.wait()

    each(z_in, 0, loaded)
    each(y_in, 0, loaded)
    last = 2 * (NZ - 1)
    for t in range(1, NZ):
        ready = 2 * ((t - 1) // 2 + 1)
        final = t == NZ - 1
        if not final:
            for d in range(2):
                arrived(z_copy, d, 0, t, NZ)
        if t > 1:
            each(z_in, t - 1, loaded)
        if t == 1:
            for copy in near_x:
                copy.wait_recv()
            for copy in near_line:
                copy.start()
        elif t == 2:
            for copy in near_line:
                copy.wait_recv()
            listed.start()
            listed.wait()
            lax.fori_loop(0, SLOTS // 2, look_up, 0)
        else:
            if t % 2 == 1:
                each(y_in, t // 2, loaded)
                part_stats(0, 2 * (t - 1), ready - 2, ready)
            if t == 3:
                part_stats(0, 4, 0, 2)
            part_stats(2 * (t - 1), 2 * t, 0, ready)
        if final:
            for n in range(2, last):
                part_copy(n).start()
            for d in range(2):
                arrived(z_copy, d, 0, t, NZ)
        for d in range(2):
            arrived(z_copy, d, 1, t, NZ)
        each(z_in, t, load)
        if t % 2 == 0:
            for a in range(2):
                for d in range(2):
                    arrived(y_copy, d, a, t // 2, NY)
            each(y_in, t // 2, load)
        if t == 2:
            lax.fori_loop(SLOTS // 2, SLOTS, look_up, 0)
        elif t == 3:
            lax.fori_loop(0, SLOTS, rank, 0)
        elif t == 4:
            lax.fori_loop(0, SLOTS, put_in_order, 0)
        elif t == 5:
            lax.fori_loop(0, SLOTS, mark_same, 0)
            lax.fori_loop(0, ROWS_HERE, mark_end, 0)
        elif t == 6:
            lax.fori_loop(0, SPANS_HERE * NBR, mark_slot, 0)
    each(z_in, NZ - 1, loaded)
    part_stats(last, last + 2, 0, 2 * NY)
    for n in range(last, last + 2):
        part_copy(n).start()
    came[z] = part[z]
    for n in range(2, last + 2):
        part_copy(n).wait_recv()

    def merge(n, carry):
        source_core, span = n // CH, lax.rem(n, CH)
        sides = []
        for item in range(NBR):
            r = near_sm[z * NC + source_core, span // 2, 0, lax.rem(span, 2) * NBR + item]
            holder = r // ROWS
            sides.append(came[lax.rem(holder // NC, NZ), source_core,
                              holder // (NC * NZ) * NC + lax.rem(holder, NC)])
        peak = jnp.maximum(sides[0][0], sides[1][0])
        weights = [jnp.exp(one[0] - peak) for one in sides]
        total = weights[0] + weights[1]
        full[z, 0, n] = peak + jnp.log(total)
        full[z, 1, n] = (weights[0] * sides[0][1] + weights[1] * sides[1][1]) / total
        return carry

    lax.fori_loop(0, NC * CH, merge, 0)
    back = [
        remote(full.at[z], full.at[z], full_s.at[s - 1], full_r.at[s - 1], index_of(y, z + s, core))
        for s in range(1, NZ)
    ]
    for copy in back:
        copy.start()
    for copy in back:
        copy.wait_recv()
    for copy in local:
        copy.wait()
    for copy in near_x + near_line + sibling + back:
        copy.wait_send()
    for n in range(2, last + 2):
        part_copy(n).wait_send()
    for d in range(2):
        for a in range(2):
            for t in range(NZ - 1):
                z_copy(d, a, t).wait_send()
            for t in range(NY - 1):
                y_copy(d, a, t).wait_send()


def gather(q, g, k, v, lists):
    sem = pltpu.SemaphoreType.DMA
    vmem = pl.BlockSpec(memory_space=pltpu.VMEM)
    part_shape = (NZ, NC, OWNERS_HERE, 2, PAIRS, HEAD)
    near_shape = (SOURCES, NX, 1, 128)
    near_count = NX - 1 + SOURCES - 1
    return pl.pallas_call(
        gather_kernel,
        out_shape=(
            jax.ShapeDtypeStruct((NZ, NC, CH, SPAN, HALF), bf16),
            jax.ShapeDtypeStruct((NZ, NC, CH, SPAN, HALF), bf16),
            jax.ShapeDtypeStruct((NY, NC, ROWS, NLEN, HALF), bf16),
            jax.ShapeDtypeStruct((NY, NC, ROWS, NLEN, HALF), bf16),
            jax.ShapeDtypeStruct((SLOTS,), jnp.int32),
            jax.ShapeDtypeStruct((SLOTS,), jnp.int32),
            jax.ShapeDtypeStruct((SLOTS,), jnp.int32),
            jax.ShapeDtypeStruct((SLOTS,), jnp.int32),
            jax.ShapeDtypeStruct((ROWS_HERE,), jnp.int32),
            jax.ShapeDtypeStruct((SPANS_HERE * NBR,), jnp.int32),
            jax.ShapeDtypeStruct(STAT_SHAPE, f32),
        ),
        in_specs=[ANY] * 4 + [vmem],
        out_specs=(ANY,) * 4 + (SMEM,) * 6 + (vmem,),
        scratch_shapes=[
            pltpu.VMEM((SOURCES, CH, SPAN, HALF), bf16),
            pltpu.VMEM((SOURCES, CH, SPAN, HALF), bf16),
            pltpu.VMEM((OWNERS_HERE, ROWS, NLEN, HALF), bf16),
            pltpu.VMEM((OWNERS_HERE, ROWS, NLEN, HALF), bf16),
            pltpu.VMEM(near_shape, jnp.int32),
            pltpu.SMEM(near_shape, jnp.int32),
            pltpu.SMEM((SLOTS,), jnp.int32),
            pltpu.SMEM((SLOTS,), jnp.int32),
            pltpu.VMEM(part_shape, f32),
            pltpu.VMEM(part_shape, f32),
            sem((4,)),
            sem((4,)),
            sem((4,)),
            sem((2, 2, NZ - 1)),
            sem((2, 2, NZ - 1)),
            sem((2, 2, NY - 1)),
            sem((2, 2, NY - 1)),
            sem((near_count,)),
            sem((near_count,)),
            sem,
            sem((2, 2, NZ)),
            sem((2, 2, NY)),
            sem((2 * NZ - 2,)),
            sem((2 * NZ - 2,)),
            sem((NZ - 1,)),
            sem((NZ - 1,)),
        ],
        compiler_params=pltpu.CompilerParams(
            collective_id=0, has_side_effects=True, vmem_limit_bytes=56 * 2**20),
        name="gather_blocks",
    )(q, g, k, v, lists)


SMEM = pl.BlockSpec(memory_space=pltpu.SMEM)
STAT_SHAPE = (NZ, 2, NC * CH, PAIRS, HEAD)


def grads_kernel(qa, ga, ka, va, table, hits, order, same, ends, slots, stat, dq, dk, dv,
                 qv, gv, k0, v0, k1, v1, dk_sum, dv_sum, y_own, y_in, parts, z_out, z_in,
                 span_l, row_l, zs, zr, ys, yr, out_s, out_r, out_l):
    y, z, core = place()
    sib = index_of(y, z, 1 - core)
    z_peer = (index_of(y, z + 1, core), index_of(y, z - 1, core))
    y_peer = (index_of(y + 1, z, core), index_of(y - 1, z, core))
    side = (1 - core, core)
    units = [(p, t, d) for p in range(PAIRS) for t in range(NY) for d in range(2)]
    row_bufs = ((k0, v0), (k1, v1))

    def z_block(d, t):
        return lax.rem(z + (2 * d - 1) * (1 + t) + NZ, NZ)

    def y_block(d, t):
        return lax.rem(y + (2 * d - 1) * (1 + t) + NY, NY)

    def span_load(p):
        columns = slice(p * PAIR, (p + 1) * PAIR)
        return [
            pltpu.make_async_copy(src.at[:, :, :, :, columns], dst, span_l.at[p, n])
            for n, (src, dst) in enumerate(((qa, qv), (ga, gv)))
        ]

    def row_load(u):
        p, t, d = units[u]
        columns = slice(p * PAIR, (p + 1) * PAIR)
        return [
            pltpu.make_async_copy(
                src.at[y_block(d, t), side[d], :, :, columns], row_bufs[u % 2][n], row_l.at[u, n])
            for n, src in enumerate((ka, va))
        ]

    for copy in row_load(0) + span_load(0):
        copy.start()
    greet((sib,) + z_peer + y_peer)
    dk_sum[0] = jnp.zeros((NLEN, PAIR), f32)
    dv_sum[0] = jnp.zeros((NLEN, PAIR), f32)
    for p in range(PAIRS):
        parts[p, SLOTS] = jnp.zeros((SPAN, PAIR), bf16)

    def compute(u):
        p, t, d = units[u]
        keys_ref, values_ref = row_bufs[u % 2]
        owner = y_block(d, t) * NC + side[d]
        for copy in row_load(u):
            copy.wait()
        if u + 1 < len(units):
            for copy in row_load(u + 1):
                copy.start()

        def slot(n):
            source = order[owner * SOURCES + n]
            found = table[source * OWNERS_HERE + owner]
            empty = 1 - hits[source * OWNERS_HERE + owner]
            span, row = found // ROWS, lax.rem(found, ROWS)
            local = lax.rem(source, NC) * CH + span
            log_total = stat[source // NC, 0, local][p:p + 1] + empty.astype(f32) * 1e30
            delta = stat[source // NC, 1, local][p:p + 1]
            keys, values = keys_ref[row], values_ref[row]
            queries = diagonal(qv[source // NC, lax.rem(source, NC), span])
            grads = diagonal(gv[source // NC, lax.rem(source, NC), span])
            probs = jnp.exp(dot(keys, queries, NT) * SCALE - log_total)
            grad_p = dot(values, grads, NT)
            grad_s = (probs * (grad_p - delta) * SCALE).astype(bf16)
            more = dot(grad_s, keys, TN)
            more = jnp.concatenate([more[:SPAN, :HEAD], more[SPAN:, HEAD:]], axis=1)
            return dot(probs.astype(bf16), grads, NN), dot(grad_s, queries, NN), more.astype(bf16)

        def step(i, carry):
            results = [slot(i * UNROLL + n) for n in range(UNROLL)]
            for n, (dv_part, dk_part, more) in enumerate(results):
                at_n = i * UNROLL + n
                parts[p, owner * SOURCES + at_n] = more
                go_on = same[owner * SOURCES + at_n].astype(f32)
                dv_sum[at_n + 1] = dv_part + go_on * dv_sum[at_n]
                dk_sum[at_n + 1] = dk_part + go_on * dk_sum[at_n]
            return carry

        lax.fori_loop(0, SOURCES // UNROLL, step, 0)

        def settle(row, carry):
            at_row = ends[owner * ROWS + row]
            y_own[p, d, t, 0, row] = dk_sum[at_row].astype(bf16)
            y_own[p, d, t, 1, row] = dv_sum[at_row].astype(bf16)
            return carry

        lax.fori_loop(0, ROWS, settle, 0)
        if t == 0:
            y_copy(p, d, 0).start()

    def y_copy(p, d, t):
        src = y_own.at[p, d, 0] if t == 0 else y_in.at[p, d, t - 1]
        return remote(src, y_in.at[p, d, t], ys.at[p, d, t], yr.at[p, d, t], y_peer[d])

    def z_copy(p, d, t):
        src = z_out.at[p, d] if t == 0 else z_in.at[p, d, t - 1]
        return remote(src, z_in.at[p, d, t], zs.at[p, d, t], zr.at[p, d, t], z_peer[d])

    def finish(p, which):
        columns = pl.ds(pl.multiple_of(core * HALF + p * PAIR, PAIR), PAIR)
        out = (dk, dv, dq)[which].at[:, :, columns]
        if which < 2:
            src = (y_in.at[p, 0, NY - 2, which], y_in.at[p, 1, NY - 2, which])
        else:
            src = (z_in.at[p, 0, NZ - 2], z_in.at[p, 1, NZ - 2])
        return (
            remote(src[0], out, out_s.at[p, which], out_r.at[p, which], sib),
            pltpu.make_async_copy(src[1], out, out_l.at[p, which]),
        )

    def y_step(p, t):
        for d in range(2):
            y_copy(p, d, t).wait_recv()

            def add(n, carry):
                for a in range(2):
                    total = y_in[p, d, t, a, n].astype(f32) + y_own[p, d, t + 1, a, n].astype(f32)
                    y_in[p, d, t, a, n] = total.astype(bf16)
                return carry

            lax.fori_loop(0, ROWS, add, 0)
            if t < NY - 2:
                y_copy(p, d, t + 1).start()
            else:
                finish(p, 0)[d].start()
                finish(p, 1)[d].start()

    def span_part(p, d, t, n):
        item = ((z_block(d, t) * NC + side[d]) * CH + n) * NBR
        return parts[p, slots[item]].astype(f32) + parts[p, slots[item + 1]].astype(f32)

    def z_begin(p):
        for d in range(2):
            def fill(n, carry):
                z_out[p, d, n] = span_part(p, d, 0, n).astype(bf16)
                return carry

            lax.fori_loop(0, CH, fill, 0)
            z_copy(p, d, 0).start()

    def z_step(p, t):
        for d in range(2):
            z_copy(p, d, t).wait_recv()

            def add(n, carry):
                z_in[p, d, t, n] = (z_in[p, d, t, n].astype(f32) + span_part(p, d, t + 1, n)).astype(bf16)
                return carry

            lax.fori_loop(0, CH, add, 0)
            if t < NZ - 2:
                z_copy(p, d, t + 1).start()
            else:
                finish(p, 2)[d].start()

    for copy in span_load(0):
        copy.wait()
    for u in range(6):
        compute(u)
    y_step(0, 0)
    compute(6)
    compute(7)
    for copy in span_load(1):
        copy.start()
    z_begin(0)
    for copy in span_load(1):
        copy.wait()
    compute(8)
    z_step(0, 0)
    compute(9)
    z_step(0, 1)
    y_step(0, 1)
    compute(10)
    z_step(0, 2)
    compute(11)
    z_step(0, 3)
    compute(12)
    z_step(0, 4)
    compute(13)
    z_step(0, 5)
    y_step(0, 2)
    compute(14)
    z_step(0, 6)
    compute(15)
    z_begin(1)
    y_step(1, 0)
    z_step(1, 0)
    z_step(1, 1)
    z_step(1, 2)
    y_step(1, 1)
    z_step(1, 3)
    z_step(1, 4)
    z_step(1, 5)
    z_step(1, 6)
    y_step(1, 2)
    for p in range(PAIRS):
        for which in range(3):
            there, here = finish(p, which)
            there.wait()
            here.wait()
        for d in range(2):
            for t in range(NZ - 1):
                z_copy(p, d, t).wait_send()
            for t in range(NY - 1):
                y_copy(p, d, t).wait_send()


def grads(qa, ga, ka, va, tables, stat):
    sem = pltpu.SemaphoreType.DMA
    vmem = pltpu.VMEM
    rows = vmem((ROWS, NLEN, PAIR), bf16)
    return pl.pallas_call(
        grads_kernel,
        out_shape=(
            jax.ShapeDtypeStruct((CH, SPAN, WIDE), bf16),
            jax.ShapeDtypeStruct((ROWS, NLEN, WIDE), bf16),
            jax.ShapeDtypeStruct((ROWS, NLEN, WIDE), bf16),
        ),
        in_specs=[ANY] * 4 + [SMEM] * len(tables) + [pl.BlockSpec(memory_space=vmem)],
        out_specs=(ANY,) * 3,
        scratch_shapes=[
            vmem((NZ, NC, CH, SPAN, PAIR), bf16),
            vmem((NZ, NC, CH, SPAN, PAIR), bf16),
            rows,
            rows,
            rows,
            rows,
            vmem((SOURCES + 1, NLEN, PAIR), f32),
            vmem((SOURCES + 1, NLEN, PAIR), f32),
            vmem((PAIRS, 2, NY, 2, ROWS, NLEN, PAIR), bf16),
            vmem((PAIRS, 2, NY - 1, 2, ROWS, NLEN, PAIR), bf16),
            vmem((PAIRS, SLOTS + 1, SPAN, PAIR), bf16),
            vmem((PAIRS, 2, CH, SPAN, PAIR), bf16),
            vmem((PAIRS, 2, NZ - 1, CH, SPAN, PAIR), bf16),
            sem((PAIRS, 2)),
            sem((PAIRS * NY * 2, 2)),
            sem((PAIRS, 2, NZ - 1)),
            sem((PAIRS, 2, NZ - 1)),
            sem((PAIRS, 2, NY - 1)),
            sem((PAIRS, 2, NY - 1)),
            sem((PAIRS, 3)),
            sem((PAIRS, 3)),
            sem((PAIRS, 3)),
        ],
        compiler_params=pltpu.CompilerParams(
            collective_id=1, has_side_effects=True, vmem_limit_bytes=62 * 2**20),
        name="grads_and_sums",
    )(qa, ga, ka, va, *tables, stat)


def per_device(queries, out_grad, row_keys, row_values, neighbours):
    few = neighbours.size
    lists = jnp.pad(neighbours.reshape(1, few), ((0, 0), (0, 128 - few)))
    qa, ga, ka, va, *tables, full = gather(queries, out_grad, row_keys, row_values, lists)
    return grads(qa, ga, ka, va, tables, full)


def solution(mesh):
    in_specs = (
        P("seq", None, "mp"),
        P("seq", None, "mp"),
        P("seq", None, "mp"),
        P("seq", None, "mp"),
        P(("seq", "mp"), None),
    )
    out_specs = (P("seq", None, "mp"), P("seq", None, "mp"), P("seq", None, "mp"))
    return jax.shard_map(
        per_device, mesh=mesh, in_specs=in_specs, out_specs=out_specs, check_vma=False
    )
```

time: 414 us -> 378 us (0.913); the launches traced: 408 us -> 378 us
  Pallas kernels: 398 us -> 370 us
    pallas_call x1, Pallas kernels: 209 us -> 188 us  [gather(): pl.pallas_call(gather_kernel, out_shape=(jax.ShapeDtypeStruct((NZ, NC, CH...]
    pallas_call x2 -> x1, Pallas kernels: 188 us -> 182 us  [grads(): pl.pallas_call(grads_kernel, out_shape=(jax.ShapeDtypeStruct((CH, SPAN, W...]
    unnamed x3 -> x7, local copies, waits for them, and re-layouts: 8.42 us -> 6.08 us
where the time goes in v4:
time: 378 us
  Pallas kernels  370 us (98%)
  local copies, waits for them, and re-layouts  7.36 us (2%)
    pallas_call x1, Pallas kernels, gather(): pl.pallas_call(gather_kernel, out_shape=(jax.ShapeDtypeStruct((NZ, NC, CH...  188 us
    pallas_call x1, Pallas kernels, grads(): pl.pallas_call(grads_kernel, out_shape=(jax.ShapeDtypeStruct((CH, SPAN, W...  182 us

profile of v4, /device:TPU:1, one launch (start us, length us, event | category | flops | bytes accessed | tf_op | source)
XLA Modules:
  0.0 377.7 jit_solution(1447180686936622705)
XLA Ops:
  0.6 0.8 reshape.9
  1.4 0.5 pad.4.lists
  1.9 188.0 %gather_blocks.1 = (bf16[8,2,8,64,512]{4,3,2,1,0:T(8,128)(2,1)}, bf16[8,2,8,64,512]{4,3,2,1,0:T(8,128)(2,1)}, bf16[4,2,8,128,512]{4,3,2,1,0:T(8,128)(2,1)}, bf16...) custom-call(bf16[8,64,1024]{2,1,0:T(8,128)(2,1)} %q.1, ...), custom_call_target="tpu_custom_call" | custom-call | tf_op jit(solution)/shard_map/gather_blocks/pallas_call | solution.py:388
  189.9 181.7 %grads_and_sums.1 = (bf16[8,64,1024]{2,1,0:T(8,128)(2,1)}, bf16[8,128,1024]{2,1,0:T(8,128)(2,1)}, bf16[8,128,1024]{2,1,0:T(8,128)(2,1)}) custom-call(bf16[8,2,8,64,512]{4,3,2,1,0:T(8,128)(2,1)} %get-tuple-element.14.qa, bf16[8,2,8,64,512]{4,3,2,1,0:T(8,128)(2,1)} %get-tuple-element.15.ga, bf16[4,2,8,128,512]{4,3,2,1,0:T(8,128)(2,1)} %get-tuple-element.16.ka, ...), custom_call_target="tpu_custom_call" | custom-call | tf_op jit(solution)/shard_map/grads_and_sums/pallas_call | solution.py:654
  371.6 0.0 copy-start.1
  371.6 2.4 copy.11
  374.0 0.0 copy-done.1
  374.0 0.0 copy-start
  374.0 1.3 copy.12
  375.4 1.0 copy-done
  376.4 1.3 copy.13
Async XLA Ops:
  371.6 2.4 copy-start.1
  374.0 2.3 copy-start

commit v5 on v4

--- a/solution.py
+++ b/solution.py
@@ -6,7 +6,7 @@
 from jax.sharding import PartitionSpec as P
 
 HEAD = 128
-UNROLL = 4
+UNROLL = 8
 SPAN = 64
 NLEN = 128
 NBR = 2
@@ -314,9 +314,13 @@
                 part_copy(n).start()
             for d in range(2):
                 arrived(z_copy, d, 0, t, NZ)
+                z_in(d, 0, t).start()
         for d in range(2):
             arrived(z_copy, d, 1, t, NZ)
-        each(z_in, t, load)
+            if final:
+                z_in(d, 1, t).start()
+        if not final:
+            each(z_in, t, load)
         if t % 2 == 0:
             for a in range(2):
                 for d in range(2):
@@ -341,11 +345,11 @@
     for n in range(2, last + 2):
         part_copy(n).wait_recv()
 
-    def merge(n, carry):
-        source_core, span = n // CH, lax.rem(n, CH)
+    def merge(n):
+        source_core, span = n // CH, n % CH
         sides = []
         for item in range(NBR):
-            r = near_sm[z * NC + source_core, span // 2, 0, lax.rem(span, 2) * NBR + item]
+            r = near_sm[z * NC + source_core, span // 2, 0, (span % 2) * NBR + item]
             holder = r // ROWS
             sides.append(came[lax.rem(holder // NC, NZ), source_core,
                               holder // (NC * NZ) * NC + lax.rem(holder, NC)])
@@ -354,9 +358,9 @@
         total = weights[0] + weights[1]
         full[z, 0, n] = peak + jnp.log(total)
         full[z, 1, n] = (weights[0] * sides[0][1] + weights[1] * sides[1][1]) / total
-        return carry
-
-    lax.fori_loop(0, NC * CH, merge, 0)
+
+    for n in range(NC * CH):
+        merge(n)
     back = [
         remote(full.at[z], full.at[z], full_s.at[s - 1], full_r.at[s - 1], index_of(y, z + s, core))
         for s in range(1, NZ)
@@ -608,29 +612,29 @@
     for copy in span_load(1):
         copy.wait()
     compute(8)
+    compute(9)
+    compute(10)
     z_step(0, 0)
-    compute(9)
+    y_step(0, 1)
+    compute(11)
+    compute(12)
+    compute(13)
     z_step(0, 1)
-    y_step(0, 1)
-    compute(10)
-    z_step(0, 2)
-    compute(11)
-    z_step(0, 3)
-    compute(12)
-    z_step(0, 4)
-    compute(13)
-    z_step(0, 5)
-    y_step(0, 2)
     compute(14)
-    z_step(0, 6)
     compute(15)
     z_begin(1)
+    z_step(0, 2)
     y_step(1, 0)
     z_step(1, 0)
+    z_step(0, 3)
+    y_step(0, 2)
     z_step(1, 1)
+    z_step(0, 4)
     z_step(1, 2)
+    z_step(0, 5)
     y_step(1, 1)
     z_step(1, 3)
+    z_step(0, 6)
     z_step(1, 4)
     z_step(1, 5)
     z_step(1, 6)

time: 378 us -> 359 us (0.950)
  Pallas kernels: 370 us -> 351 us
    pallas_call x1, Pallas kernels: 182 us -> 164 us  [grads(): pl.pallas_call(grads_kernel, out_shape=(jax.ShapeDtypeStruct((CH, SPAN, W...]
where the time goes in v5:
time: 359 us
  Pallas kernels  351 us (98%)
  local copies, waits for them, and re-layouts  7.36 us (2%)
    pallas_call x1, Pallas kernels, gather(): pl.pallas_call(gather_kernel, out_shape=(jax.ShapeDtypeStruct((NZ, NC, CH...  188 us
    pallas_call x1, Pallas kernels, grads(): pl.pallas_call(grads_kernel, out_shape=(jax.ShapeDtypeStruct((CH, SPAN, W...  164 us

profile of v5, /device:TPU:1, one launch (start us, length us, event | category | flops | bytes accessed | tf_op | source)
XLA Modules:
  0.0 359.2 jit_solution(978991797712991738)
XLA Ops:
  0.6 0.8 reshape.9
  1.4 0.5 pad.4.lists
  1.9 187.5 %gather_blocks.1 = (bf16[8,2,8,64,512]{4,3,2,1,0:T(8,128)(2,1)}, bf16[8,2,8,64,512]{4,3,2,1,0:T(8,128)(2,1)}, bf16[4,2,8,128,512]{4,3,2,1,0:T(8,128)(2,1)}, bf16...) custom-call(bf16[8,64,1024]{2,1,0:T(8,128)(2,1)} %q.1, ...), custom_call_target="tpu_custom_call" | custom-call | tf_op jit(solution)/shard_map/gather_blocks/pallas_call | solution.py:392
  189.4 163.6 %grads_and_sums.1 = (bf16[8,64,1024]{2,1,0:T(8,128)(2,1)}, bf16[8,128,1024]{2,1,0:T(8,128)(2,1)}, bf16[8,128,1024]{2,1,0:T(8,128)(2,1)}) custom-call(bf16[8,2,8,64,512]{4,3,2,1,0:T(8,128)(2,1)} %get-tuple-element.14.qa, bf16[8,2,8,64,512]{4,3,2,1,0:T(8,128)(2,1)} %get-tuple-element.15.ga, bf16[4,2,8,128,512]{4,3,2,1,0:T(8,128)(2,1)} %get-tuple-element.16.ka, ...), custom_call_target="tpu_custom_call" | custom-call | tf_op jit(solution)/shard_map/grads_and_sums/pallas_call | solution.py:658
  353.1 0.0 copy-start.1
  353.1 2.4 copy.11
  355.5 0.0 copy-done.1
  355.5 0.0 copy-start
  355.5 1.3 copy.12
  356.8 1.0 copy-done
  357.9 1.3 copy.13
Async XLA Ops:
  353.1 2.4 copy-start.1
  355.5 2.3 copy-start
